TPU v7x, 256 devices: a whole 4x4x8 slice. The times are simulated.
256 devices in a mesh: ctx: 64 (over y, x, z_hi), dp: 4 (over z_lo, core).
Axes of the slice: x: 4, y: 4, z: 8 (z_hi: 4, z_lo: 2; z = z_hi * 2 + z_lo), core: 2. Of those that a mesh axis runs over, the one named last changes fastest.
Arguments:
- token_ids: int32 [4, 8192], P('dp', 'ctx'), may hold values from 0 to 511
- embedding: bfloat16 [512, 2048], replicated, may hold values from -6 to 6
- in_gate: bfloat16 [4, 8192, 2048], P('dp', 'ctx'), may hold values from -6 to 6
- teacher_gate: bfloat16 [4, 8192, 2048], P('dp', 'ctx'), may hold values from -6 to 6
- student_gate: bfloat16 [4, 8192, 2048], P('dp', 'ctx'), may hold values from -6 to 6
- teacher_filter: bfloat16 [8192, 2048], P('ctx')
- student_filter: bfloat16 [8192, 2048], P('ctx')
Outputs:
- student_out: bfloat16 [4, 8192, 2048], P('dp', 'ctx')
- filter_grad: float32 [8192, 2048], P('ctx')
All inputs are finite; a program needn't handle non-finite values.
Results may differ from a plain program's by a relative error of at most 0.022.
Values may be sent and summed in bfloat16 or wider, within the bound.
No kernel may reach another device: no remote copies, remote signals or barrier semaphores. Data moves between devices by JAX's collectives and lax.ppermute only.
A program may use at most 128 MiB of HBM per device.

v0:
```python
import math

import jax
import jax.numpy as jnp
from jax import lax
from jax.sharding import PartitionSpec as P

BRISK = lax.Precision.HIGH


def phase_table(first, second, period):
    prod = first[:, None] * second[None, :] % period
    return prod.astype(jnp.float32) * (2.0 * math.pi / period)


def table_dot(table, data, form):
    upper = table.astype(jnp.bfloat16)
    lower = (table - upper.astype(jnp.float32)).astype(jnp.bfloat16)
    first = jnp.einsum(form, upper, data, preferred_element_type=jnp.float32)
    return first + jnp.einsum(form, lower, data, preferred_element_type=jnp.float32)


def block_section(blocks, j_global, span_len):
    block_count = blocks.shape[0]
    freq_idx = jnp.arange(2 * block_count, dtype=jnp.int32)
    angles = phase_table(freq_idx, jnp.arange(block_count, dtype=jnp.int32), 2 * block_count)
    dft_table = jnp.concatenate([jnp.cos(angles), -jnp.sin(angles)], axis=0)
    stacked = table_dot(dft_table, blocks, "fa,asc->fsc")
    stacked = stacked.reshape((2, 2 * block_count) + blocks.shape[1:])
    twiddle = phase_table(freq_idx, j_global, span_len)[:, :, None]
    cosines, sines = (jnp.cos(twiddle), jnp.sin(twiddle))
    part_re = stacked[0] * cosines + stacked[1] * sines
    part_im = stacked[1] * cosines - stacked[0] * sines
    return (part_re.astype(jnp.bfloat16), part_im.astype(jnp.bfloat16))


def row_section(part_re, part_im):
    length = part_re.shape[1]
    positions = jnp.arange(length, dtype=jnp.int32)
    angles = phase_table(positions, positions, length)
    cosines, sines = (jnp.cos(angles), jnp.sin(angles))
    rotation = jnp.concatenate(
        [jnp.concatenate([cosines, sines], axis=1), jnp.concatenate([-sines, cosines], axis=1)],
        axis=0,
    )
    stacked = jnp.concatenate([part_re, part_im], axis=1)
    result = table_dot(rotation, stacked, "kj,fjc->fkc")
    return (result[:, :length], result[:, length:])


def row_inverse(spec_re, spec_im, freq_global, span_len, wire_type):
    length = spec_re.shape[1]
    positions = jnp.arange(length, dtype=jnp.int32)
    angles = phase_table(positions, positions, length)
    cosines, sines = (jnp.cos(angles), jnp.sin(angles))
    rotation = jnp.concatenate(
        [jnp.concatenate([cosines, -sines], axis=1), jnp.concatenate([sines, cosines], axis=1)],
        axis=0,
    )
    stacked = jnp.concatenate([spec_re, spec_im], axis=1)
    result = jnp.einsum(
        "kj,fjc->fkc", rotation, stacked, precision=BRISK, preferred_element_type=jnp.float32
    )
    wave_re = result[:, :length]
    wave_im = result[:, length:]
    twiddle = phase_table(freq_global, positions, span_len)[:, :, None]
    tw_cos, tw_sin = (jnp.cos(twiddle), jnp.sin(twiddle))
    part_re = (wave_re * tw_cos - wave_im * tw_sin).astype(wire_type)
    part_im = (wave_im * tw_cos + wave_re * tw_sin).astype(wire_type)
    return (part_re, part_im)


def block_inverse(part_re, part_im, span_len):
    freq_count = part_re.shape[0]
    block_count = freq_count // 2
    angles = phase_table(
        jnp.arange(block_count, dtype=jnp.int32),
        jnp.arange(freq_count, dtype=jnp.int32),
        freq_count,
    )
    dft_table = jnp.concatenate([jnp.cos(angles), -jnp.sin(angles)], axis=1) / span_len
    stacked = jnp.concatenate([part_re, part_im], axis=0)
    if stacked.dtype == jnp.bfloat16:
        return table_dot(dft_table, stacked, "af,fsc->asc")
    return jnp.einsum(
        "af,fsc->asc", dft_table, stacked, precision=BRISK, preferred_element_type=jnp.float32
    )


def body(token_ids, embedding, in_gate, teacher_gate, student_gate, teacher_filter, student_filter):
    ctx_count = lax.axis_size("ctx")
    ctx_pos = lax.axis_index("ctx")
    dp_count = lax.axis_size("dp")
    tok_count = token_ids.shape[1]
    vocab_size = embedding.shape[0]
    seq_len = tok_count * ctx_count
    span_len = 2 * seq_len
    one_hot = (token_ids[0][:, None] == jnp.arange(vocab_size, dtype=jnp.int32)[None, :]).astype(
        jnp.bfloat16
    )
    values = jnp.dot(one_hot, embedding, preferred_element_type=jnp.float32)
    mixed = (in_gate[0].astype(jnp.float32) * values).astype(jnp.bfloat16)

    def forward(signal):
        spread = lax.all_to_all(signal[None], "ctx", split_axis=1, concat_axis=0, tiled=True)
        sub_count = spread.shape[1]
        j_global = ctx_pos * sub_count + jnp.arange(sub_count, dtype=jnp.int32)
        part_re, part_im = block_section(spread, j_global, span_len)
        part_re, part_im = (
            lax.all_to_all(part_re, "ctx", split_axis=0, concat_axis=1, tiled=True),
            lax.all_to_all(part_im, "ctx", split_axis=0, concat_axis=1, tiled=True),
        )
        return row_section(part_re, part_im)

    def inverse(spec_re, spec_im, exact):
        local_freq = spec_re.shape[0]
        freq_global = ctx_pos * local_freq + jnp.arange(local_freq, dtype=jnp.int32)
        if exact:
            part_re, part_im = row_inverse(spec_re, spec_im, freq_global, span_len, jnp.float32)
            part_re, part_im = (
                lax.all_to_all(
                    part_re.astype(jnp.bfloat16), "ctx", split_axis=1, concat_axis=0, tiled=True
                ).astype(part_re.dtype),
                lax.all_to_all(
                    part_im.astype(jnp.bfloat16), "ctx", split_axis=1, concat_axis=0, tiled=True
                ).astype(part_im.dtype),
            )
            blocks = block_inverse(part_re, part_im, span_len)
            return lax.all_to_all(
                blocks.astype(jnp.bfloat16), "ctx", split_axis=0, concat_axis=1, tiled=True
            ).astype(blocks.dtype)[0]
        part_re, part_im = row_inverse(spec_re, spec_im, freq_global, span_len, jnp.bfloat16)
        part_re, part_im = (
            lax.all_to_all(part_re, "ctx", split_axis=1, concat_axis=0, tiled=True),
            lax.all_to_all(part_im, "ctx", split_axis=1, concat_axis=0, tiled=True),
        )
        blocks = block_inverse(part_re, part_im, span_len).astype(jnp.bfloat16)
        return lax.all_to_all(blocks, "ctx", split_axis=0, concat_axis=1, tiled=True)[0]

    local_in, gate_teach, gate_stud = (mixed, teacher_gate[0], student_gate[0])
    filt_teach, filt_stud = (teacher_filter, student_filter)
    width = local_in.shape[-1]
    filters = jnp.concatenate([filt_teach, filt_stud], axis=-1)
    in_re, in_im = forward(local_in)
    filt_re, filt_im = forward(filters)
    both_re = jnp.concatenate([in_re, in_re], axis=-1)
    both_im = jnp.concatenate([in_im, in_im], axis=-1)
    conv_both = inverse(
        both_re * filt_re - both_im * filt_im, both_re * filt_im + both_im * filt_re, False
    )
    conv_t = conv_both[:, :width]
    conv_s = conv_both[:, width:]
    teach = gate_teach.astype(jnp.float32) * conv_t.astype(jnp.float32)
    stud = gate_stud.astype(jnp.float32) * conv_s.astype(jnp.float32)
    grad_out = (gate_stud.astype(jnp.float32) * (stud - teach)).astype(jnp.bfloat16)
    grad_re, grad_im = forward(grad_out)
    lag_grad = inverse(grad_re * in_re + grad_im * in_im, grad_im * in_re - grad_re * in_im, True)
    student = stud.astype(jnp.bfloat16)
    summed = lax.psum(lag_grad.astype(jnp.bfloat16), "dp").astype(jnp.float32)
    filter_grad = summed * (dp_count * seq_len) ** (-0.5)
    return (student[None], filter_grad)


def solution(mesh):
    placed = (
        P("dp", "ctx"),
        P(),
        P("dp", "ctx", None),
        P("dp", "ctx", None),
        P("dp", "ctx", None),
        P("ctx", None),
        P("ctx", None),
    )
    return jax.shard_map(
        body,
        mesh=mesh,
        in_specs=placed,
        out_specs=(P("dp", "ctx", None), P("ctx", None)),
        check_vma=False,
    )
```

profile of v0, /device:TPU:1, one launch (start us, length us, event | category | flops | bytes accessed | tf_op | source)
XLA Modules:
  0.0 649.3 jit_solution(3269433655213169726)
XLA Ops:
  16.6 15.7 %all-to-all-start = ((bf16[64,2,2048]{2,1,0:T(2,128)(2,1)}), bf16[64,2,2048]{2,1,0:T(2,128)(2,1)}, u32[]{:S(2)}, u32[]{:S(2)}) async-start(bf16[64,2,2048]{2,1,0:T(2,128)(2,1)} %reshape.184), calls=%async_computation | async-start | bytes 1048576 | tf_op jit(solution)/shard_map/all_to_all | solution.py:105
  34.8 7.0 %reduce.7 = bf16[128,4096]{1,0:T(8,128)(2,1)S(1)} reduce(bf16[128,1,4096]{2,1,0:T(2,128)(2,1)S(1)} %bitcast.132, bf16[]{:T(256)} %broadcast.271), dimensions={1}, to_apply=%bitcast.127.reduce_sub_computation | reduce | bytes 2097154
  43.3 6.8 %all-to-all-done = bf16[64,2,2048]{2,1,0:T(2,128)(2,1)} async-done(((bf16[64,2,2048]{2,1,0:T(2,128)(2,1)}), bf16[64,2,2048]{2,1,0:T(2,128)(2,1)}, u32[]{:S(2)}, u32[]{:S(2)}) %all-to-all-start) | async-done | bytes 524320 | tf_op jit(solution)/shard_map/all_to_all | solution.py:105
  50.1 7.2 %all-to-all-start.3 = ((bf16[64,2,4096]{2,1,0:T(2,128)(2,1)}), bf16[64,2,4096]{2,1,0:T(2,128)(2,1)S(1)}, u32[]{:S(2)}, u32[]{:S(2)}) async-start(bf16[64,2,4096]{2,1,0:T(2,128)(2,1)} %reshape.186), calls=%async_computation.3 | async-start | bytes 2097152 | tf_op jit(solution)/shard_map/all_to_all | solution.py:105
  69.1 18.2 %all-to-all-done.3 = bf16[64,2,4096]{2,1,0:T(2,128)(2,1)S(1)} async-done(((bf16[64,2,4096]{2,1,0:T(2,128)(2,1)}), bf16[64,2,4096]{2,1,0:T(2,128)(2,1)S(1)}, u32[]{:S(2)}, u32[]{:S(2)}) %all-to-all-start.3) | async-done | bytes 1048608 | tf_op jit(solution)/shard_map/all_to_all | solution.py:105
  87.3 6.9 %all-to-all-start.1 = ((bf16[128,2,2048]{2,1,0:T(2,128)(2,1)}), bf16[128,2,2048]{2,1,0:T(2,128)(2,1)}, u32[]{:S(2)}, u32[]{:S(2)}) async-start(bf16[128,2,2048]{2,1,0:T(2,128)(2,1)} %copy.90), calls=%async_computation.1 | async-start | bytes 2097152 | tf_op jit(solution)/shard_map/all_to_all | solution.py:110
  97.4 6.2 bitcast_reduce_fusion
  104.3 14.6 %all-to-all-done.1 = bf16[128,2,2048]{2,1,0:T(2,128)(2,1)} async-done(((bf16[128,2,2048]{2,1,0:T(2,128)(2,1)}), bf16[128,2,2048]{2,1,0:T(2,128)(2,1)}, u32[]{:S(2)}, u32[]{:S(2)}) %all-to-all-start.1) | async-done | bytes 1048608 | tf_op jit(solution)/shard_map/all_to_all | solution.py:110
  118.9 7.4 %all-to-all-start.2 = ((bf16[128,2,2048]{2,1,0:T(2,128)(2,1)}), bf16[128,2,2048]{2,1,0:T(2,128)(2,1)S(1)}, u32[]{:S(2)}, u32[]{:S(2)}) async-start(bf16[128,2,2048]{2,1,0:T(2,128)(2,1)} %copy.92), calls=%async_computation.2 | async-start | bytes 2097152 | tf_op jit(solution)/shard_map/all_to_all | solution.py:111
  136.1 10.1 %all-to-all-done.2 = bf16[128,2,2048]{2,1,0:T(2,128)(2,1)S(1)} async-done(((bf16[128,2,2048]{2,1,0:T(2,128)(2,1)}), bf16[128,2,2048]{2,1,0:T(2,128)(2,1)S(1)}, u32[]{:S(2)}, u32[]{:S(2)}) %all-to-all-start.2) | async-done | bytes 1048608 | tf_op jit(solution)/shard_map/all_to_all | solution.py:111
  146.2 6.3 all-to-all-start.4
  157.5 24.2 %all-to-all-done.4 = bf16[128,2,4096]{2,1,0:T(2,128)(2,1)S(1)} async-done(((bf16[128,2,4096]{2,1,0:T(2,128)(2,1)}), bf16[128,2,4096]{2,1,0:T(2,128)(2,1)S(1)}, u32[]{:S(2)}, u32[]{:S(2)}) %all-to-all-start.4) | async-done | bytes 2097184 | tf_op jit(solution)/shard_map/all_to_all | solution.py:110
  181.7 6.0 all-to-all-start.5
  211.8 10.2 %all-to-all-done.5 = bf16[128,2,4096]{2,1,0:T(2,128)(2,1)} async-done(((bf16[128,2,4096]{2,1,0:T(2,128)(2,1)}), bf16[128,2,4096]{2,1,0:T(2,128)(2,1)}, u32[]{:S(2)}, u32[]{:S(2)}) %all-to-all-start.5) | async-done | bytes 2097184 | tf_op jit(solution)/shard_map/all_to_all | solution.py:111
  222.0 5.3 copy.150
  248.6 6.9 %all-to-all-start.6 = ((bf16[2,128,4096]{2,0,1:T(2,128)(2,1)}), bf16[2,128,4096]{2,0,1:T(2,128)(2,1)S(1)}, u32[]{:S(2)}, u32[]{:S(2)}) async-start(bf16[2,128,4096]{2,0,1:T(2,128)(2,1)} %copy.105), calls=%async_computation.6 | async-start | bytes 4194304 | tf_op jit(solution)/shard_map/all_to_all | solution.py:134
  255.5 6.2 copy.107
  261.7 20.7 %all-to-all-done.6 = bf16[2,128,4096]{2,0,1:T(2,128)(2,1)S(1)} async-done(((bf16[2,128,4096]{2,0,1:T(2,128)(2,1)}), bf16[2,128,4096]{2,0,1:T(2,128)(2,1)S(1)}, u32[]{:S(2)}, u32[]{:S(2)}) %all-to-all-start.6) | async-done | bytes 2097184 | tf_op jit(solution)/shard_map/all_to_all | solution.py:134
  282.4 7.0 %all-to-all-start.7 = ((bf16[2,128,4096]{2,0,1:T(2,128)(2,1)}), bf16[2,128,4096]{2,0,1:T(2,128)(2,1)}, u32[]{:S(2)}, u32[]{:S(2)}) async-start(bf16[2,128,4096]{2,0,1:T(2,128)(2,1)} %copy.107), calls=%async_computation.7 | async-start | bytes 4194304 | tf_op jit(solution)/shard_map/all_to_all | solution.py:135
  297.6 32.6 %all-to-all-done.7 = bf16[2,128,4096]{2,0,1:T(2,128)(2,1)} async-done(((bf16[2,128,4096]{2,0,1:T(2,128)(2,1)}), bf16[2,128,4096]{2,0,1:T(2,128)(2,1)}, u32[]{:S(2)}, u32[]{:S(2)}) %all-to-all-start.7) | async-done | bytes 2097184 | tf_op jit(solution)/shard_map/all_to_all | solution.py:135
  330.2 5.3 copy.108
  345.4 36.9 %all_to_all.219 = bf16[64,2,4096]{2,1,0:T(2,128)(2,1)S(1)} all-to-all(bf16[64,2,4096]{2,1,0:T(2,128)(2,1)S(1)} %copy.109), channel_id=1, replica_groups=mesh['ctx'=64,'dp'=4] {'ctx'}, dimensions={0} | all-to-all | bytes 2097152 | tf_op jit(solution)/shard_map/all_to_all | solution.py:138
  388.8 27.1 %all_to_all.220 = bf16[64,2,2048]{2,1,0:T(2,128)(2,1)S(1)} all-to-all(bf16[64,2,2048]{2,1,0:T(2,128)(2,1)S(1)} %reshape.188), channel_id=1, replica_groups=mesh['ctx'=64,'dp'=4] {'ctx'}, dimensions={0} | all-to-all | bytes 1048576 | tf_op jit(solution)/shard_map/all_to_all | solution.py:105
  424.2 7.9 %all-to-all-start.10 = ((bf16[128,2,2048]{2,1,0:T(2,128)(2,1)}), bf16[128,2,2048]{2,1,0:T(2,128)(2,1)S(1)}, u32[]{:S(2)}, u32[]{:S(2)}) async-start(bf16[128,2,2048]{2,1,0:T(2,128)(2,1)} %copy.113), calls=%async_computation.10 | async-start | bytes 2097152 | tf_op jit(solution)/shard_map/all_to_all | solution.py:110
  434.3 16.9 %all-to-all-done.10 = bf16[128,2,2048]{2,1,0:T(2,128)(2,1)S(1)} async-done(((bf16[128,2,2048]{2,1,0:T(2,128)(2,1)}), bf16[128,2,2048]{2,1,0:T(2,128)(2,1)S(1)}, u32[]{:S(2)}, u32[]{:S(2)}) %all-to-all-start.10) | async-done | bytes 1048608 | tf_op jit(solution)/shard_map/all_to_all | solution.py:110
  459.3 16.2 %all-to-all-done.11 = bf16[128,2,2048]{2,1,0:T(2,128)(2,1)S(1)} async-done(((bf16[128,2,2048]{2,1,0:T(2,128)(2,1)}), bf16[128,2,2048]{2,1,0:T(2,128)(2,1)S(1)}, u32[]{:S(2)}, u32[]{:S(2)}) %all-to-all-start.11) | async-done | bytes 1048608 | tf_op jit(solution)/shard_map/all_to_all | solution.py:111
  486.8 6.3 all-to-all-start.12
  495.1 18.6 %all-to-all-done.12 = bf16[2,128,2048]{2,0,1:T(2,128)(2,1)S(1)} async-done(((bf16[2,128,2048]{2,0,1:T(2,128)(2,1)}), bf16[2,128,2048]{2,0,1:T(2,128)(2,1)S(1)}, u32[]{:S(2)}, u32[]{:S(2)}) %all-to-all-start.12) | async-done | bytes 1048608 | tf_op jit(solution)/shard_map/all_to_all | solution.py:121
  513.7 7.2 %all-to-all-start.13 = ((bf16[2,128,2048]{2,0,1:T(2,128)(2,1)}), bf16[2,128,2048]{2,0,1:T(2,128)(2,1)S(1)}, u32[]{:S(2)}, u32[]{:S(2)}) async-start(bf16[2,128,2048]{2,0,1:T(2,128)(2,1)} %copy.121), calls=%async_computation.13 | async-start | bytes 2097152 | tf_op jit(solution)/shard_map/all_to_all | solution.py:124
  523.1 16.5 %all-to-all-done.13 = bf16[2,128,2048]{2,0,1:T(2,128)(2,1)S(1)} async-done(((bf16[2,128,2048]{2,0,1:T(2,128)(2,1)}), bf16[2,128,2048]{2,0,1:T(2,128)(2,1)S(1)}, u32[]{:S(2)}, u32[]{:S(2)}) %all-to-all-start.13) | async-done | bytes 1048608 | tf_op jit(solution)/shard_map/all_to_all | solution.py:124
  544.5 18.6 %all_to_all.221 = bf16[64,2,2048]{2,1,0:T(2,128)(2,1)S(1)} all-to-all(bf16[64,2,2048]{2,1,0:T(2,128)(2,1)S(1)} %copy.123), channel_id=1, replica_groups=mesh['ctx'=64,'dp'=4] {'ctx'}, dimensions={0} | all-to-all | bytes 1048576 | tf_op jit(solution)/shard_map/all_to_all | solution.py:129
  564.2 75.9 %all-reduce.2.cloned.1.call-done = bf16[128,2048]{1,0:T(8,128)(2,1)} async-done(((bf16[128,2048]{1,0:T(8,128)(2,1)}), bf16[128,2048]{1,0:T(8,128)(2,1)}) %all-reduce.2.cloned.1.call-update) | async-done | bytes 524304 | tf_op jit(solution)/shard_map/psum | solution.py:159
  (121 shorter events, 155.5 us)
Async XLA Ops:
  7.2 1.6 copy-start
  8.8 23.5 %copy-start.10 = (bf16[128,2048]{1,0:T(8,128)(2,1)S(1)}, bf16[128,2048]{1,0:T(8,128)(2,1)}, u32[]{:S(2)}) copy-start(bf16[128,2048]{1,0:T(8,128)(2,1)} %param.13) | copy-start | bytes 1572868
  8.8 23.5 %copy-start.11 = (bf16[128,2048]{1,0:T(8,128)(2,1)S(1)}, bf16[128,2048]{1,0:T(8,128)(2,1)}, u32[]{:S(2)}) copy-start(bf16[128,2048]{1,0:T(8,128)(2,1)} %param.12) | copy-start | bytes 1572868
  16.6 33.5 %all-to-all-start = ((bf16[64,2,2048]{2,1,0:T(2,128)(2,1)}), bf16[64,2,2048]{2,1,0:T(2,128)(2,1)}, u32[]{:S(2)}, u32[]{:S(2)}) async-start(bf16[64,2,2048]{2,1,0:T(2,128)(2,1)} %reshape.184), calls=%async_computation | async-start | bytes 1048576 | tf_op jit(solution)/shard_map/all_to_all | solution.py:105
  50.1 37.2 %all-to-all-start.3 = ((bf16[64,2,4096]{2,1,0:T(2,128)(2,1)}), bf16[64,2,4096]{2,1,0:T(2,128)(2,1)S(1)}, u32[]{:S(2)}, u32[]{:S(2)}) async-start(bf16[64,2,4096]{2,1,0:T(2,128)(2,1)} %reshape.186), calls=%async_computation.3 | async-start | bytes 2097152 | tf_op jit(solution)/shard_map/all_to_all | solution.py:105
  87.3 31.5 %all-to-all-start.1 = ((bf16[128,2,2048]{2,1,0:T(2,128)(2,1)}), bf16[128,2,2048]{2,1,0:T(2,128)(2,1)}, u32[]{:S(2)}, u32[]{:S(2)}) async-start(bf16[128,2,2048]{2,1,0:T(2,128)(2,1)} %copy.90), calls=%async_computation.1 | async-start | bytes 2097152 | tf_op jit(solution)/shard_map/all_to_all | solution.py:110
  118.9 27.3 %all-to-all-start.2 = ((bf16[128,2,2048]{2,1,0:T(2,128)(2,1)}), bf16[128,2,2048]{2,1,0:T(2,128)(2,1)S(1)}, u32[]{:S(2)}, u32[]{:S(2)}) async-start(bf16[128,2,2048]{2,1,0:T(2,128)(2,1)} %copy.92), calls=%async_computation.2 | async-start | bytes 2097152 | tf_op jit(solution)/shard_map/all_to_all | solution.py:111
  146.2 35.5 %all-to-all-start.4 = ((bf16[128,2,4096]{2,1,0:T(2,128)(2,1)}), bf16[128,2,4096]{2,1,0:T(2,128)(2,1)S(1)}, u32[]{:S(2)}, u32[]{:S(2)}) async-start(bf16[128,2,4096]{2,1,0:T(2,128)(2,1)} %copy.99), calls=%async_computation.4 | async-start | bytes 4194304 | tf_op jit(solution)/shard_map/all_to_all | solution.py:110
  181.7 10.0 %copy-start.6 = (bf16[128,2,4096]{2,1,0:T(2,128)(2,1)}, bf16[128,2,4096]{2,1,0:T(2,128)(2,1)S(1)}, u32[]{:S(2)}) copy-start(bf16[128,2,4096]{2,1,0:T(2,128)(2,1)S(1)} %all-to-all-done.4) | copy-start | bytes 6291460
  181.7 40.3 %all-to-all-start.5 = ((bf16[128,2,4096]{2,1,0:T(2,128)(2,1)}), bf16[128,2,4096]{2,1,0:T(2,128)(2,1)}, u32[]{:S(2)}, u32[]{:S(2)}) async-start(bf16[128,2,4096]{2,1,0:T(2,128)(2,1)} %copy.101), calls=%async_computation.5 | async-start | bytes 4194304 | tf_op jit(solution)/shard_map/all_to_all | solution.py:111
  200.3 3.4 copy-start.2
  200.3 3.4 copy-start.7
  231.6 3.7 copy-start.4
  235.3 1.6 copy-start.8
  235.3 2.2 copy-start.9
  248.6 33.8 %all-to-all-start.6 = ((bf16[2,128,4096]{2,0,1:T(2,128)(2,1)}), bf16[2,128,4096]{2,0,1:T(2,128)(2,1)S(1)}, u32[]{:S(2)}, u32[]{:S(2)}) async-start(bf16[2,128,4096]{2,0,1:T(2,128)(2,1)} %copy.105), calls=%async_computation.6 | async-start | bytes 4194304 | tf_op jit(solution)/shard_map/all_to_all | solution.py:134
  282.4 47.8 %all-to-all-start.7 = ((bf16[2,128,4096]{2,0,1:T(2,128)(2,1)}), bf16[2,128,4096]{2,0,1:T(2,128)(2,1)}, u32[]{:S(2)}, u32[]{:S(2)}) async-start(bf16[2,128,4096]{2,0,1:T(2,128)(2,1)} %copy.107), calls=%async_computation.7 | async-start | bytes 4194304 | tf_op jit(solution)/shard_map/all_to_all | solution.py:135
  339.9 3.4 copy-start.5
  344.3 38.5 %copy-start.12 = (bf16[1,128,2048]{2,1,0:T(8,128)(2,1)S(1)}, bf16[1,128,2048]{2,1,0:T(8,128)(2,1)}, u32[]{:S(2)}) copy-start(bf16[1,128,2048]{2,1,0:T(8,128)(2,1)} %param.10) | copy-start | bytes 1572868
  344.3 38.5 %copy-start.13 = (bf16[1,128,2048]{2,1,0:T(8,128)(2,1)S(1)}, bf16[1,128,2048]{2,1,0:T(8,128)(2,1)}, u32[]{:S(2)}) copy-start(bf16[1,128,2048]{2,1,0:T(8,128)(2,1)} %param.11) | copy-start | bytes 1572868
  424.2 26.9 %all-to-all-start.10 = ((bf16[128,2,2048]{2,1,0:T(2,128)(2,1)}), bf16[128,2,2048]{2,1,0:T(2,128)(2,1)S(1)}, u32[]{:S(2)}, u32[]{:S(2)}) async-start(bf16[128,2,2048]{2,1,0:T(2,128)(2,1)} %copy.113), calls=%async_computation.10 | async-start | bytes 2097152 | tf_op jit(solution)/shard_map/all_to_all | solution.py:110
  451.2 24.3 %all-to-all-start.11 = ((bf16[128,2,2048]{2,1,0:T(2,128)(2,1)}), bf16[128,2,2048]{2,1,0:T(2,128)(2,1)S(1)}, u32[]{:S(2)}, u32[]{:S(2)}) async-start(bf16[128,2,2048]{2,1,0:T(2,128)(2,1)} %copy.115), calls=%async_computation.11 | async-start | bytes 2097152 | tf_op jit(solution)/shard_map/all_to_all | solution.py:111
  479.5 2.2 copy-start.3
  486.8 26.9 %all-to-all-start.12 = ((bf16[2,128,2048]{2,0,1:T(2,128)(2,1)}), bf16[2,128,2048]{2,0,1:T(2,128)(2,1)S(1)}, u32[]{:S(2)}, u32[]{:S(2)}) async-start(bf16[2,128,2048]{2,0,1:T(2,128)(2,1)} %copy.119), calls=%async_computation.12 | async-start | bytes 2097152 | tf_op jit(solution)/shard_map/all_to_all | solution.py:121
  513.7 26.0 %all-to-all-start.13 = ((bf16[2,128,2048]{2,0,1:T(2,128)(2,1)}), bf16[2,128,2048]{2,0,1:T(2,128)(2,1)S(1)}, u32[]{:S(2)}, u32[]{:S(2)}) async-start(bf16[2,128,2048]{2,0,1:T(2,128)(2,1)} %copy.121), calls=%async_computation.13 | async-start | bytes 2097152 | tf_op jit(solution)/shard_map/all_to_all | solution.py:124
  520.9 119.2 %all-reduce.2.cloned.1.call-start = ((), (), s32[]{:S(2)}) async-start(), calls=%async_computation.15 | async-start | bytes 1048576 | tf_op jit(solution)/shard_map/psum | solution.py:159
  540.4 101.9 %copy-start.1 = (bf16[512,2048]{1,0:T(8,128)(2,1)S(1)}, bf16[512,2048]{1,0:T(8,128)(2,1)}, u32[]{:S(2)}) copy-start(bf16[512,2048]{1,0:T(8,128)(2,1)} %param.8) | copy-start | bytes 6291460
Sparse Core Ops, SparseCore 0:
  564.3 75.7 all-reduce.1
where the time goes:
time: 656 us; the launch traced here: 649 us
  waiting for transfers between devices  282 us (43%)
  local copies, waits for them, and re-layouts  124 us (19%)
  starting transfers between devices  89.6 us (14%)
  blocking collectives  82.6 us (13%)
  matrix products  28.8 us (4%)
  other arithmetic  27.5 us (4%)
  between operations  14.9 us (2%)
    psum x1, waiting for transfers between devices, body(): summed = lax.psum(lag_grad.astype(jnp.bfloat16), 'dp').astype(jnp.float32)  75.9 us
    all_to_all x3, waiting for transfers between devices, forward(): lax.all_to_all(part_re, 'ctx', split_axis=0, concat_axis=1, tiled=True)  55.6 us
    all_to_all x1, blocking collectives, inverse(): lax.all_to_all(blocks, 'ctx', split_axis=0, concat_axis=1, tiled=True)[0]  36.9 us
    all_to_all x3, waiting for transfers between devices, forward(): lax.all_to_all(part_im, 'ctx', split_axis=0, concat_axis=1, tiled=True)  36.5 us
    all_to_all x1, waiting for transfers between devices, inverse(): lax.all_to_all(part_im, 'ctx', split_axis=1, concat_axis=0, tiled=True)  32.6 us
    all_to_all x1, blocking collectives, forward(): lax.all_to_all(signal[None], 'ctx', split_axis=1, concat_axis=0, tiled=True)  27.1 us
    all_to_all x2, waiting for transfers between devices, forward(): lax.all_to_all(signal[None], 'ctx', split_axis=1, concat_axis=0, tiled=True)  25 us
    all_to_all x2, starting transfers between devices, forward(): lax.all_to_all(signal[None], 'ctx', split_axis=1, concat_axis=0, tiled=True)  22.9 us
  transfers between devices with their start and end apart: 13, of which 13 were waited for; matrix products, arithmetic and copies ran while one was open for 13% of the time, Pallas kernels for 0%

commit v1 on v0

v1 whole, which is shorter than its diff:
```python
import functools
import math

import jax
import jax.numpy as jnp
import numpy as np
from jax import lax
from jax.experimental import pallas as pl
from jax.experimental.pallas import tpu as pltpu
from jax.sharding import PartitionSpec as P

SUB = 8
LANES = 128
CHUNK = 256
MIB = 1 << 20


def tables(blocks, inner):
    span = 2 * blocks * inner
    freq = np.arange(blocks, dtype=np.float64) + 0.5
    pos = np.arange(blocks, dtype=np.float64)
    lane = np.arange(inner, dtype=np.float64)
    angle = 2.0 * np.pi * ((freq[:, None] * pos[None, :]) % (2 * blocks)) / (2 * blocks)
    both = np.stack([np.cos(angle), -np.sin(angle)])
    spread = np.einsum("rka,im->rkiam", both, np.eye(SUB))
    spread = spread.reshape(2, blocks * SUB // CHUNK, CHUNK, blocks * SUB)
    first = spread.transpose(1, 0, 2, 3).reshape(2 * blocks * SUB, blocks * SUB)
    turn = 2.0 * np.pi * (freq[:, None] * lane[None, :]) / span
    turn = np.repeat(np.stack([np.cos(turn), np.sin(turn)]), SUB, axis=1)
    angle = 2.0 * np.pi * ((lane[:, None] * lane[None, :]) % inner) / inner
    cosines, sines = np.cos(angle), np.sin(angle)
    second = np.block([[cosines, -sines], [sines, cosines]])
    bf = jnp.bfloat16
    return (
        jnp.asarray(first, bf),
        jnp.asarray(first.T * (2.0 / span), bf),
        jnp.asarray(turn, jnp.float32),
        jnp.asarray(second, bf),
        jnp.asarray(second.T, bf),
    )


def dot(a, b):
    return jnp.dot(a, b, preferred_element_type=jnp.float32)


def dot_nt(a, b):
    return lax.dot_general(a, b, (((1,), (1,)), ((), ())), preferred_element_type=jnp.float32)


def unit(size):
    rows = lax.broadcasted_iota(jnp.int32, (size, size), 0)
    cols = lax.broadcasted_iota(jnp.int32, (size, size), 1)
    return (rows == cols).astype(jnp.float32).astype(jnp.bfloat16)


def pack_kernel(tok_ref, emb_ref, in_ref, teach_ref, stud_ref, ft_ref, fs_ref, out_ref):
    vocab, width = emb_ref.shape
    toks = tok_ref.shape[1]
    rows = lax.broadcasted_iota(jnp.int32, (vocab, toks), 0)
    one_hot = (rows == tok_ref[...]).astype(jnp.float32).astype(jnp.bfloat16)
    values = lax.dot_general(
        one_hot, emb_ref[...], (((0,), (0,)), ((), ())), preferred_element_type=jnp.float32
    )
    mixed = (in_ref[0].astype(jnp.float32) * values).astype(jnp.bfloat16)
    teacher = lax.axis_index("dp") < lax.axis_size("dp") // 2
    taps = jnp.where(teacher, ft_ref[...], fs_ref[...])
    eye = unit(width)
    parts = [
        dot_nt(eye, x).reshape(width // SUB, SUB, toks)
        for x in (mixed, stud_ref[0], teach_ref[0], taps)
    ]
    out_ref[...] = jnp.concatenate(parts, axis=1).astype(jnp.bfloat16)


def pack(token_ids, embedding, in_gate, teacher_gate, student_gate, teacher_filter, student_filter):
    vocab, channels = embedding.shape
    toks = token_ids.shape[1]
    width = 256
    gate = pl.BlockSpec((1, toks, width), lambda g: (0, 0, g))
    taps = pl.BlockSpec((toks, width), lambda g: (0, g))
    return pl.pallas_call(
        pack_kernel,
        grid=(channels // width,),
        in_specs=[
            pl.BlockSpec((1, toks), lambda g: (0, 0)),
            pl.BlockSpec((vocab, width), lambda g: (0, g)),
            gate,
            gate,
            gate,
            taps,
            taps,
        ],
        out_specs=pl.BlockSpec((width // SUB, 4 * SUB, toks), lambda g: (g, 0, 0)),
        out_shape=jax.ShapeDtypeStruct((channels // SUB, 4 * SUB, toks), jnp.bfloat16),
        compiler_params=pltpu.CompilerParams(vmem_limit_bytes=32 * MIB),
    )(token_ids, embedding, in_gate, teacher_gate, student_gate, teacher_filter, student_filter)


def filter_kernel(
    seqs, blocks, scale, in_ref, t1_ref, t1i_ref, turn_ref, t2_ref, t2i_ref, out_ref,
    x_ref, spec_ref, wave_ref, stud_ref, grad_ref, lag_ref,
):
    bf, f32 = jnp.bfloat16, jnp.float32
    toks = in_ref.shape[2]
    full = blocks * SUB
    chunks = full // CHUNK
    per = CHUNK // SUB

    def source(seq, chunk, part):
        data = in_ref[pl.ds(seq * blocks + chunk * per, per)].astype(f32)
        return data[:, part * SUB:(part + 1) * SUB, :].reshape(CHUNK, toks)

    def lanes(n):
        return pl.ds(n * toks, toks)

    def gather(chunk, carry):
        rows = pl.ds(pl.multiple_of(chunk * CHUNK, CHUNK), CHUNK)
        for d in range(seqs):
            x_ref[rows, lanes(d)] = source(d, chunk, 0).astype(bf)
        for f in range(2):
            x_ref[rows, lanes(seqs + f)] = source(f * (seqs // 2), chunk, 3).astype(bf)
        return carry

    lax.fori_loop(0, chunks, gather, 0)

    def forward(chunk, data, count):
        rows = pl.ds(pl.multiple_of(chunk * 2 * CHUNK, CHUNK), 2 * CHUNK)
        turn = pl.ds(pl.multiple_of(chunk * CHUNK, CHUNK), CHUNK)
        cosines, sines = turn_ref[0, turn, :], turn_ref[1, turn, :]
        out = dot(t1_ref[rows, :], data)
        parts = []
        for n in range(count):
            re = out[:CHUNK, n * toks:(n + 1) * toks]
            im = out[CHUNK:, n * toks:(n + 1) * toks]
            parts.append(
                jnp.concatenate([re * cosines + im * sines, im * cosines - re * sines], axis=1)
                .astype(bf)
            )
        return dot(jnp.concatenate(parts, axis=0), t2_ref[...])

    def back(chunk, prod):
        turn = pl.ds(pl.multiple_of(chunk * CHUNK, CHUNK), CHUNK)
        cosines, sines = turn_ref[0, turn, :], turn_ref[1, turn, :]
        re, im = prod[:, :toks], prod[:, toks:]
        return re * cosines - im * sines, im * cosines + re * sines

    def convolve(chunk, carry):
        rows = pl.ds(pl.multiple_of(chunk * CHUNK, CHUNK), CHUNK)
        upper = pl.ds(pl.multiple_of(chunk * 2 * CHUNK, CHUNK), CHUNK)
        lower = pl.ds(pl.multiple_of(chunk * 2 * CHUNK + CHUNK, CHUNK), CHUNK)
        spec = forward(chunk, x_ref[...], seqs + 2)
        for d in range(seqs):
            spec_ref[d, rows, :] = spec[d * CHUNK:(d + 1) * CHUNK]
        for f in range(2):
            taps = spec[(seqs + f) * CHUNK:(seqs + f + 1) * CHUNK]
            tr, ti = taps[:, :toks], taps[:, toks:]
            prods = []
            for d in range(seqs):
                ur = spec[d * CHUNK:(d + 1) * CHUNK, :toks]
                ui = spec[d * CHUNK:(d + 1) * CHUNK, toks:]
                prods.append(
                    jnp.concatenate([ur * tr - ui * ti, ur * ti + ui * tr], axis=1).astype(bf)
                )
            waves = dot(jnp.concatenate(prods, axis=0), t2i_ref[...])
            for d in range(seqs):
                re, im = back(chunk, waves[d * CHUNK:(d + 1) * CHUNK])
                wave_ref[upper, lanes(f * seqs + d)] = re.astype(bf)
                wave_ref[lower, lanes(f * seqs + d)] = im.astype(bf)
        return carry

    lax.fori_loop(0, chunks, convolve, 0)

    def gate(chunk, carry):
        rows = pl.ds(pl.multiple_of(chunk * CHUNK, CHUNK), CHUNK)
        conv = dot(t1i_ref[rows, :], wave_ref[...])
        conv = conv.astype(bf).astype(f32)
        for d in range(seqs):
            conv_t = conv[:, d * toks:(d + 1) * toks]
            conv_s = conv[:, (seqs + d) * toks:(seqs + d + 1) * toks]
            gate_s = source(d, chunk, 1)
            stud = gate_s * conv_s
            stud_ref[rows, lanes(d)] = stud
            grad = gate_s * (stud - source(d, chunk, 2) * conv_t)
            grad_ref[rows, lanes(d)] = grad.astype(bf)
        return carry

    lax.fori_loop(0, chunks, gate, 0)

    def correlate(chunk, carry):
        rows = pl.ds(pl.multiple_of(chunk * CHUNK, CHUNK), CHUNK)
        upper = pl.ds(pl.multiple_of(chunk * 2 * CHUNK, CHUNK), CHUNK)
        lower = pl.ds(pl.multiple_of(chunk * 2 * CHUNK + CHUNK, CHUNK), CHUNK)
        spec = forward(chunk, grad_ref[...], seqs)
        sum_re = jnp.zeros((CHUNK, toks), f32)
        sum_im = jnp.zeros((CHUNK, toks), f32)
        for d in range(seqs):
            gr = spec[d * CHUNK:(d + 1) * CHUNK, :toks]
            gi = spec[d * CHUNK:(d + 1) * CHUNK, toks:]
            ur, ui = spec_ref[d, rows, :toks], spec_ref[d, rows, toks:]
            sum_re += gr * ur + gi * ui
            sum_im += gi * ur - gr * ui
        total = jnp.concatenate([sum_re, sum_im], axis=1)
        high = total.astype(bf)
        low = (total - high.astype(f32)).astype(bf)
        waves = dot(jnp.concatenate([high, low], axis=0), t2i_ref[...])
        re, im = back(chunk, waves[:CHUNK] + waves[CHUNK:])
        for piece, place in ((re, upper), (im, lower)):
            high = piece.astype(bf)
            lag_ref[place, lanes(0)] = high
            lag_ref[place, lanes(1)] = (piece - high.astype(f32)).astype(bf)
        return carry

    lax.fori_loop(0, chunks, correlate, 0)

    def finish(chunk, carry):
        rows = pl.ds(pl.multiple_of(chunk * CHUNK, CHUNK), CHUNK)
        lags = dot(t1i_ref[rows, :], lag_ref[...])
        lags = ((lags[:, :toks] + lags[:, toks:]) * scale).reshape(per, SUB, toks)
        for d in range(seqs):
            stud = stud_ref[rows, lanes(d)].reshape(per, SUB, toks)
            out_ref[pl.ds(d * blocks + chunk * per, per)] = jnp.concatenate(
                [stud, lags], axis=1
            ).astype(bf)
        return carry

    lax.fori_loop(0, chunks, finish, 0)


def filters(data, seqs, blocks):
    toks = data.shape[2]
    full = blocks * SUB
    scale = float(seqs * blocks * toks) ** -0.5
    bf, f32 = jnp.bfloat16, jnp.float32
    return pl.pallas_call(
        functools.partial(filter_kernel, seqs, blocks, scale),
        out_shape=jax.ShapeDtypeStruct((seqs * blocks, 2 * SUB, toks), bf),
        scratch_shapes=[
            pltpu.VMEM((full, (seqs + 2) * toks), bf),
            pltpu.VMEM((seqs, full, 2 * toks), f32),
            pltpu.VMEM((2 * full, 2 * seqs * toks), bf),
            pltpu.VMEM((full, seqs * toks), f32),
            pltpu.VMEM((full, seqs * toks), bf),
            pltpu.VMEM((2 * full, 2 * toks), bf),
        ],
        compiler_params=pltpu.CompilerParams(vmem_limit_bytes=48 * MIB),
    )(data, *tables(blocks, toks))


def unpack_kernel(in_ref, stud_ref, lag_ref):
    count, _, toks = in_ref.shape
    data = in_ref[...].astype(jnp.float32)
    eye = unit(toks)
    stud = data[:, :SUB, :].reshape(count * SUB, toks).astype(jnp.bfloat16)
    lags = data[:, SUB:, :].reshape(count * SUB, toks).astype(jnp.bfloat16)
    stud_ref[0] = dot_nt(eye, stud).astype(jnp.bfloat16)
    lag_ref[...] = dot_nt(eye, lags)


def unpack(data):
    senders, rows, toks = data.shape
    channels = senders * SUB
    width = 256
    return pl.pallas_call(
        unpack_kernel,
        grid=(channels // width,),
        in_specs=[pl.BlockSpec((width // SUB, rows, toks), lambda g: (g, 0, 0))],
        out_specs=(
            pl.BlockSpec((1, toks, width), lambda g: (0, 0, g)),
            pl.BlockSpec((toks, width), lambda g: (0, g)),
        ),
        out_shape=(
            jax.ShapeDtypeStruct((1, toks, channels), jnp.bfloat16),
            jax.ShapeDtypeStruct((toks, channels), jnp.float32),
        ),
        compiler_params=pltpu.CompilerParams(vmem_limit_bytes=32 * MIB),
    )(data)


def body(*args):
    seqs, blocks = lax.axis_size("dp"), lax.axis_size("ctx")

    def exchange(x):
        return lax.all_to_all(x, ("dp", "ctx"), split_axis=0, concat_axis=0, tiled=True)

    return unpack(exchange(filters(exchange(pack(*args)), seqs, blocks)))


def solution(mesh):
    placed = (
        P("dp", "ctx"),
        P(),
        P("dp", "ctx", None),
        P("dp", "ctx", None),
        P("dp", "ctx", None),
        P("ctx", None),
        P("ctx", None),
    )
    return jax.shard_map(
        body,
        mesh=mesh,
        in_specs=placed,
        out_specs=(P("dp", "ctx", None), P("ctx", None)),
        check_vma=False,
    )
```

time: 656 us -> 130 us (0.20)
  waiting for transfers between devices: 282 us -> 0 us
  local copies, waits for them, and re-layouts: 124 us -> 7.48 us
  starting transfers between devices: 89.6 us -> 0 us
  matrix products: 28.8 us -> 0 us
  other arithmetic: 27.5 us -> 0 us
  blocking collectives: 82.6 us -> 105 us
  Pallas kernels: 0 us -> 15.7 us
  between operations: 14.9 us -> 0.72 us
    all_to_all x12 -> x0, waiting for transfers between devices: 206 us -> none  [the longest x3 55.6 us: forward(): lax.all_to_all(part_re, 'ctx', split_axis=0, concat_axis=1, tiled=True)]
    all_to_all x12 -> x0, starting transfers between devices: 89.6 us -> none  [the longest x2 22.9 us: forward(): lax.all_to_all(signal[None], 'ctx', split_axis=1, concat_axis=0, tiled=True)]
    psum x1 -> x0, waiting for transfers between devices: 75.9 us -> none  [body(): summed = lax.psum(lag_grad.astype(jnp.bfloat16), 'dp').astype(jnp.float32)]
    all_to_all x23 -> x0, local copies, waits for them, and re-layouts: 59.2 us -> none  [the longest x6 15.8 us: forward(): lax.all_to_all(part_im, 'ctx', split_axis=0, concat_axis=1, tiled=True)]
    convert_element_type x16 -> x0, local copies, waits for them, and re-layouts: 36.9 us -> none  [the longest x6 16.9 us: block_section(): return (part_re.astype(jnp.bfloat16), part_im.astype(jnp.bfloat16))]
    dot_general x18 -> x0, matrix products: 28.8 us -> none  [the longest x7 11.7 us: table_dot(): first = jnp.einsum(form, upper, data, preferred_element_type=jnp.float32)]
    all_to_all x3 -> x2, blocking collectives: 82.6 us -> 105 us  [exchange(): lax.all_to_all(x, ('dp', 'ctx'), split_axis=0, concat_axis=0, tiled=True)]
    pallas_call x0 -> x3, Pallas kernels: none -> 15.7 us  [the longest x1 7.3 us: filters(): pl.pallas_call(functools.partial(filter_kernel, seqs, blocks, scale), out...]
  transfers between devices with their start and end apart: 13 -> 0, of which waited for: 13 -> 0; matrix products, arithmetic and copies ran while one was open for 13% -> 0% of each run, Pallas kernels for 0% -> 0%
where the time goes in v1:
time: 130 us; the launch traced here: 129 us
  blocking collectives  105 us (81%)
  Pallas kernels  15.7 us (12%)
  local copies, waits for them, and re-layouts  7.48 us (6%)
    all_to_all x2, blocking collectives, exchange(): lax.all_to_all(x, ('dp', 'ctx'), split_axis=0, concat_axis=0, tiled=True)  105 us
    unnamed x24, local copies, waits for them, and re-layouts  7.48 us
    pallas_call x1, Pallas kernels, filters(): pl.pallas_call(functools.partial(filter_kernel, seqs, blocks, scale), out...  7.3 us
    pallas_call x1, Pallas kernels, pack(): pl.pallas_call(pack_kernel, grid=(channels // width,), in_specs=[pl.Block...  4.68 us
    pallas_call x1, Pallas kernels, unpack(): pl.pallas_call(unpack_kernel, grid=(channels // width,), in_specs=[pl.Blo...  3.67 us

profile of v1, /device:TPU:1, one launch (start us, length us, event | category | flops | bytes accessed | tf_op | source)
XLA Modules:
  0.0 129.2 jit_solution(9361173120811723016)
XLA Ops:
  0.6 0.0 copy-start
  0.6 1.6 %copy-done = bf16[512,2048]{1,0:T(8,128)(2,1)S(1)} copy-done((bf16[512,2048]{1,0:T(8,128)(2,1)S(1)}, bf16[512,2048]{1,0:T(8,128)(2,1)}, u32[]{:S(2)}) %copy-start) | copy-done | bytes 2097176
  2.2 0.0 copy-start.4
  2.2 1.0 copy-done.4
  3.3 0.0 copy-start.5
  3.3 1.0 copy-done.5
  4.3 0.0 copy-start.6
  4.3 1.0 copy-done.6
  5.4 0.0 copy-start.7
  5.4 1.0 copy-done.7
  6.4 0.0 copy-start.8
  6.4 1.0 copy-done.8
  7.4 0.0 copy-start.11
  7.4 0.7 copy-done.11
  8.1 4.7 %shard_map.131 = bf16[256,32,128]{2,1,0:T(8,128)(2,1)S(1)} custom-call(s32[1,128]{1,0:T(1,128)S(1)} %copy-done.11, bf16[512,2048]{1,0:T(8,128)(2,1)S(1)} %copy-done, bf16[1,128,2048]{2,1,0:T(8,128)(2,1)S(1)} %copy-done.4, bf16[1,128,2048]{2,1,0:T(8,128)(2,1)S(1)} %copy-done.5, bf16[1,128,2048]{2,1,0:T(8,128)(2,1)S(1)} %copy-done.6, ...), custom_call_target="tpu_custom_call" | custom-call | tf_op jit(solution)/shard_map/pallas_call | solution.py:82
  12.8 0.0 copy-start.1
  12.8 0.0 copy-start.2
  12.8 0.0 copy-start.3
  12.8 0.0 copy-start.9
  12.8 0.0 copy-start.10
  12.8 68.4 %all_to_all.10.in_ref = bf16[256,32,128]{2,1,0:T(8,128)(2,1)S(1)} all-to-all(bf16[256,32,128]{2,1,0:T(8,128)(2,1)S(1)} %shard_map.131), channel_id=1, replica_groups=mesh['ctx'=64,'dp'=4] {'dp','ctx'}, dimensions={0} | all-to-all | bytes 4194304 | tf_op jit(solution)/shard_map/all_to_all | solution.py:284
  81.3 0.0 copy-done.1
  81.3 0.0 copy-done.2
  81.3 0.0 copy-done.3
  81.3 0.0 copy-done.9
  81.3 0.0 copy-done.10
  81.3 7.3 %shard_map.132 = bf16[256,16,128]{2,1,0:T(8,128)(2,1)S(1)} custom-call(bf16[256,32,128]{2,1,0:T(8,128)(2,1)S(1)} %all_to_all.10.in_ref, bf16[1024,512]{1,0:T(8,128)(2,1)S(1)} %copy-done.2, bf16[512,1024]{1,0:T(8,128)(2,1)S(1)} %copy-done.1, f32[2,512,128]{2,1,0:T(8,128)S(1)} %copy-done.3, bf16[256,256]{1,0:T(8,128)(2,1)S(1)} %copy-done.10, ...), custom_call_target="tpu_custom_call" | custom-call | tf_op jit(solution)/shard_map/pallas_call | solution.py:235
  88.6 36.9 %all_to_all.11.in_ref = bf16[256,16,128]{2,1,0:T(8,128)(2,1)S(1)} all-to-all(bf16[256,16,128]{2,1,0:T(8,128)(2,1)S(1)} %shard_map.132), channel_id=1, replica_groups=mesh['ctx'=64,'dp'=4] {'dp','ctx'}, dimensions={0} | all-to-all | bytes 2097152 | tf_op jit(solution)/shard_map/all_to_all | solution.py:284
  125.5 3.7 %shard_map.133 = (bf16[1,128,2048]{2,1,0:T(8,128)(2,1)}, f32[128,2048]{1,0:T(8,128)}) custom-call(bf16[256,16,128]{2,1,0:T(8,128)(2,1)S(1)} %all_to_all.11.in_ref), custom_call_target="tpu_custom_call" | custom-call | tf_op jit(solution)/shard_map/pallas_call | solution.py:264
Async XLA Ops:
  0.6 1.6 %copy-start = (bf16[512,2048]{1,0:T(8,128)(2,1)S(1)}, bf16[512,2048]{1,0:T(8,128)(2,1)}, u32[]{:S(2)}) copy-start(bf16[512,2048]{1,0:T(8,128)(2,1)} %emb_ref.1) | copy-start | bytes 6291460
  2.2 1.0 copy-start.4
  3.3 1.0 copy-start.5
  4.3 1.0 copy-start.6
  5.4 1.0 copy-start.7
  6.4 1.0 copy-start.8
  7.4 0.7 copy-start.11
  12.8 68.5 %copy-start.1 = (bf16[512,1024]{1,0:T(8,128)(2,1)S(1)}, bf16[512,1024]{1,0:T(8,128)(2,1)}, u32[]{:S(2)}) copy-start(bf16[512,1024]{1,0:T(8,128)(2,1)} %constant.11.clone.t1i_ref) | copy-start | bytes 3145732
  12.8 68.5 %copy-start.2 = (bf16[1024,512]{1,0:T(8,128)(2,1)S(1)}, bf16[1024,512]{1,0:T(8,128)(2,1)}, u32[]{:S(2)}) copy-start(bf16[1024,512]{1,0:T(8,128)(2,1)} %constant.10.clone.t1_ref) | copy-start | bytes 3145732
  12.8 68.5 %copy-start.3 = (f32[2,512,128]{2,1,0:T(8,128)S(1)}, f32[2,512,128]{2,1,0:T(8,128)}, u32[]{:S(2)}) copy-start(f32[2,512,128]{2,1,0:T(8,128)} %constant.12.clone.turn_ref) | copy-start | bytes 1572868
  12.8 68.4 %copy-start.9 = (bf16[256,256]{1,0:T(8,128)(2,1)S(1)}, bf16[256,256]{1,0:T(8,128)(2,1)}, u32[]{:S(2)}) copy-start(bf16[256,256]{1,0:T(8,128)(2,1)} %constant.14.clone.t2i_ref) | copy-start | bytes 393220
  12.8 68.4 %copy-start.10 = (bf16[256,256]{1,0:T(8,128)(2,1)S(1)}, bf16[256,256]{1,0:T(8,128)(2,1)}, u32[]{:S(2)}) copy-start(bf16[256,256]{1,0:T(8,128)(2,1)} %constant.13.clone.t2_ref) | copy-start | bytes 393220

commit v2 on v1

--- a/solution.py
+++ b/solution.py
@@ -10,6 +10,8 @@
 from jax.sharding import PartitionSpec as P
 
 SUB = 8
+HALF = 4
+MESSAGE = 28
 LANES = 128
 CHUNK = 256
 MIB = 1 << 20
@@ -48,53 +50,120 @@
     return lax.dot_general(a, b, (((1,), (1,)), ((), ())), preferred_element_type=jnp.float32)
 
 
+def turned(x):
+    return x.T.astype(jnp.float32)
+
+
 def unit(size):
     rows = lax.broadcasted_iota(jnp.int32, (size, size), 0)
     cols = lax.broadcasted_iota(jnp.int32, (size, size), 1)
     return (rows == cols).astype(jnp.float32).astype(jnp.bfloat16)
 
 
-def pack_kernel(tok_ref, emb_ref, in_ref, teach_ref, stud_ref, ft_ref, fs_ref, out_ref):
-    vocab, width = emb_ref.shape
+def half_turn(x):
+    return jnp.concatenate([x[:, HALF:], x[:, :HALF]], axis=1)
+
+
+def halves(upper, lower):
+    rows = lax.broadcasted_iota(jnp.int32, upper.shape, 1)
+    return jnp.where(rows < HALF, upper, lower)
+
+
+def pack_kernel(
+    width, tok_ref, emb_ref, in_ref, stud_ref, teach_ref, ft_ref, fs_ref, out_ref,
+    emb_buf, data_buf, sems,
+):
+    vocab, channels = emb_ref.shape
     toks = tok_ref.shape[1]
+    chunks = channels // width
+    pairs = width // (2 * SUB)
+    dp = lax.axis_index("dp")
+    teacher = dp < lax.axis_size("dp") // 2
+    lead = lax.rem(dp, 2) == 0
+    even = lax.rem(lax.axis_index("ctx"), 2) == 0
+
+    def copies(chunk, taps):
+        cols = pl.ds(chunk * width, width)
+        sources = (
+            (emb_ref.at[:, cols], emb_buf.at[:, cols]),
+            (in_ref.at[0, :, cols], data_buf.at[0, :, cols]),
+            (stud_ref.at[0, :, cols], data_buf.at[1, :, cols]),
+            (teach_ref.at[0, :, cols], data_buf.at[2, :, cols]),
+            (taps.at[:, cols], data_buf.at[3, :, cols]),
+        )
+        return [
+            (src, dst, sems.at[chunk, n]) for n, (src, dst) in enumerate(sources)
+        ]
+
+    for chunk in range(chunks):
+        for copy in copies(chunk, ft_ref)[:4]:
+            pltpu.make_async_copy(*copy).start()
+
+        @pl.when(teacher)
+        def _():
+            pltpu.make_async_copy(*copies(chunk, ft_ref)[4]).start()
+
+        @pl.when(jnp.logical_not(teacher))
+        def _():
+            pltpu.make_async_copy(*copies(chunk, fs_ref)[4]).start()
+
     rows = lax.broadcasted_iota(jnp.int32, (vocab, toks), 0)
-    one_hot = (rows == tok_ref[...]).astype(jnp.float32).astype(jnp.bfloat16)
-    values = lax.dot_general(
-        one_hot, emb_ref[...], (((0,), (0,)), ((), ())), preferred_element_type=jnp.float32
-    )
-    mixed = (in_ref[0].astype(jnp.float32) * values).astype(jnp.bfloat16)
-    teacher = lax.axis_index("dp") < lax.axis_size("dp") // 2
-    taps = jnp.where(teacher, ft_ref[...], fs_ref[...])
-    eye = unit(width)
-    parts = [
-        dot_nt(eye, x).reshape(width // SUB, SUB, toks)
-        for x in (mixed, stud_ref[0], teach_ref[0], taps)
-    ]
-    out_ref[...] = jnp.concatenate(parts, axis=1).astype(jnp.bfloat16)
+    one_hot = (rows == tok_ref[...]).astype(jnp.float32).T.astype(jnp.bfloat16)
+
+    for chunk in range(chunks):
+        for copy in copies(chunk, ft_ref):
+            pltpu.make_async_copy(*copy).wait()
+        cols = pl.ds(chunk * width, width)
+        values = dot(one_hot, emb_buf[:, cols])
+        mixed = (data_buf[0, :, cols].astype(jnp.float32) * values).astype(jnp.bfloat16)
+        parts = [
+            turned(x).reshape(pairs, 2, SUB, toks)
+            for x in (mixed, data_buf[1, :, cols], data_buf[2, :, cols], data_buf[3, :, cols])
+        ]
+        place = pl.ds(chunk * pairs * 2 * MESSAGE, pairs * 2 * MESSAGE)
+
+        def store(tiles):
+            out_ref[place, :] = (
+                jnp.stack(tiles, axis=1).reshape(pairs * 2 * MESSAGE, toks).astype(jnp.bfloat16)
+            )
+
+        tap_upper = jnp.where(lead, parts[3][:, 0], half_turn(parts[3][:, 0]))
+        tap_lower = jnp.where(lead, half_turn(parts[3][:, 1]), parts[3][:, 1])
+
+        @pl.when(even)
+        def _():
+            mix, stud, teach = [half_turn(x[:, 1]) for x in parts[:3]]
+            store([x[:, 0] for x in parts[:3]] + [
+                halves(tap_upper, mix), halves(mix, stud), halves(stud, teach),
+                halves(teach, tap_lower),
+            ])
+
+        @pl.when(jnp.logical_not(even))
+        def _():
+            mix, stud, teach = [half_turn(x[:, 0]) for x in parts[:3]]
+            store([
+                halves(tap_upper, mix), halves(mix, stud), halves(stud, teach),
+                halves(teach, tap_lower),
+            ] + [x[:, 1] for x in parts[:3]])
 
 
 def pack(token_ids, embedding, in_gate, teacher_gate, student_gate, teacher_filter, student_filter):
     vocab, channels = embedding.shape
     toks = token_ids.shape[1]
-    width = 256
-    gate = pl.BlockSpec((1, toks, width), lambda g: (0, 0, g))
-    taps = pl.BlockSpec((toks, width), lambda g: (0, g))
+    width = 512
+    here = pl.BlockSpec(memory_space=pl.ANY)
     return pl.pallas_call(
-        pack_kernel,
-        grid=(channels // width,),
-        in_specs=[
-            pl.BlockSpec((1, toks), lambda g: (0, 0)),
-            pl.BlockSpec((vocab, width), lambda g: (0, g)),
-            gate,
-            gate,
-            gate,
-            taps,
-            taps,
+        functools.partial(pack_kernel, width),
+        in_specs=[pl.BlockSpec(memory_space=pltpu.VMEM)] + [here] * 6,
+        out_specs=pl.BlockSpec(memory_space=pltpu.VMEM),
+        out_shape=jax.ShapeDtypeStruct((channels // SUB * MESSAGE, toks), jnp.bfloat16),
+        scratch_shapes=[
+            pltpu.VMEM((vocab, channels), jnp.bfloat16),
+            pltpu.VMEM((4, toks, channels), jnp.bfloat16),
+            pltpu.SemaphoreType.DMA((channels // width, 5)),
         ],
-        out_specs=pl.BlockSpec((width // SUB, 4 * SUB, toks), lambda g: (g, 0, 0)),
-        out_shape=jax.ShapeDtypeStruct((channels // SUB, 4 * SUB, toks), jnp.bfloat16),
-        compiler_params=pltpu.CompilerParams(vmem_limit_bytes=32 * MIB),
-    )(token_ids, embedding, in_gate, teacher_gate, student_gate, teacher_filter, student_filter)
+        compiler_params=pltpu.CompilerParams(vmem_limit_bytes=60 * MIB),
+    )(token_ids, embedding, in_gate, student_gate, teacher_gate, teacher_filter, student_filter)
 
 
 def filter_kernel(
@@ -102,24 +171,35 @@
     x_ref, spec_ref, wave_ref, stud_ref, grad_ref, lag_ref,
 ):
     bf, f32 = jnp.bfloat16, jnp.float32
-    toks = in_ref.shape[2]
+    toks = in_ref.shape[1]
     full = blocks * SUB
     chunks = full // CHUNK
     per = CHUNK // SUB
 
-    def source(seq, chunk, part):
-        data = in_ref[pl.ds(seq * blocks + chunk * per, per)].astype(f32)
-        return data[:, part * SUB:(part + 1) * SUB, :].reshape(CHUNK, toks)
+    def received(seq, chunk):
+        place = pl.multiple_of((seq * blocks + chunk * per) * MESSAGE, per * MESSAGE)
+        data = in_ref[pl.ds(place, per * MESSAGE), :].astype(f32)
+        return data.reshape(per // 2, 2 * MESSAGE // SUB, SUB, toks)
+
+    def source(data, part):
+        return jnp.stack([data[:, part], data[:, part + HALF]], axis=1).reshape(CHUNK, toks)
 
     def lanes(n):
         return pl.ds(n * toks, toks)
 
     def gather(chunk, carry):
         rows = pl.ds(pl.multiple_of(chunk * CHUNK, CHUNK), CHUNK)
-        for d in range(seqs):
-            x_ref[rows, lanes(d)] = source(d, chunk, 0).astype(bf)
+        taps = []
+        for d in range(seqs):
+            data = received(d, chunk)
+            x_ref[rows, lanes(d)] = source(data, 0).astype(bf)
+            taps.append(data[:, HALF - 1])
         for f in range(2):
-            x_ref[rows, lanes(seqs + f)] = source(f * (seqs // 2), chunk, 3).astype(bf)
+            lead, other = taps[2 * f:2 * f + 2]
+            tile = jnp.stack(
+                [halves(lead, half_turn(other)), halves(half_turn(lead), other)], axis=1
+            )
+            x_ref[rows, lanes(seqs + f)] = tile.reshape(CHUNK, toks).astype(bf)
         return carry
 
     lax.fori_loop(0, chunks, gather, 0)
@@ -178,10 +258,11 @@
         for d in range(seqs):
             conv_t = conv[:, d * toks:(d + 1) * toks]
             conv_s = conv[:, (seqs + d) * toks:(seqs + d + 1) * toks]
-            gate_s = source(d, chunk, 1)
+            data = received(d, chunk)
+            gate_s = source(data, 1)
             stud = gate_s * conv_s
             stud_ref[rows, lanes(d)] = stud
-            grad = gate_s * (stud - source(d, chunk, 2) * conv_t)
+            grad = gate_s * (stud - source(data, 2) * conv_t)
             grad_ref[rows, lanes(d)] = grad.astype(bf)
         return carry
 
@@ -228,7 +309,7 @@
 
 
 def filters(data, seqs, blocks):
-    toks = data.shape[2]
+    toks = data.shape[1]
     full = blocks * SUB
     scale = float(seqs * blocks * toks) ** -0.5
     bf, f32 = jnp.bfloat16, jnp.float32
@@ -260,7 +341,7 @@
 def unpack(data):
     senders, rows, toks = data.shape
     channels = senders * SUB
-    width = 256
+    width = 512
     return pl.pallas_call(
         unpack_kernel,
         grid=(channels // width,),
@@ -283,7 +364,10 @@
     def exchange(x):
         return lax.all_to_all(x, ("dp", "ctx"), split_axis=0, concat_axis=0, tiled=True)
 
-    return unpack(exchange(filters(exchange(pack(*args)), seqs, blocks)))
+    sent = pack(*args)
+    toks = sent.shape[1]
+    got = exchange(sent.reshape(seqs * blocks, MESSAGE // HALF, HALF, toks))
+    return unpack(exchange(filters(got.reshape(sent.shape), seqs, blocks)))
 
 
 def solution(mesh):

time: 130 us -> 115 us (0.88)
  local copies, waits for them, and re-layouts: 7.48 us -> 0.03 us
  blocking collectives: 105 us -> 99.9 us
  Pallas kernels: 15.7 us -> 14.3 us
    unnamed x24 -> x10, local copies, waits for them, and re-layouts: 7.48 us -> 0.03 us
    all_to_all x2, blocking collectives: 105 us -> 99.9 us  [exchange(): lax.all_to_all(x, ('dp', 'ctx'), split_axis=0, concat_axis=0, tiled=True)]
    pallas_call x1, Pallas kernels: 3.67 us -> 2.13 us  [unpack(): pl.pallas_call(unpack_kernel, grid=(channels // width,), in_specs=[pl.Blo...]
where the time goes in v2:
time: 115 us
  blocking collectives  99.9 us (87%)
  Pallas kernels  14.3 us (12%)
    all_to_all x2, blocking collectives, exchange(): lax.all_to_all(x, ('dp', 'ctx'), split_axis=0, concat_axis=0, tiled=True)  99.9 us
    pallas_call x1, Pallas kernels, filters(): pl.pallas_call(functools.partial(filter_kernel, seqs, blocks, scale), out...  7.3 us
    pallas_call x1, Pallas kernels, pack(): pl.pallas_call(functools.partial(pack_kernel, width), in_specs=[pl.BlockS...  4.9 us

profile of v2, /device:TPU:1, one launch (start us, length us, event | category | flops | bytes accessed | tf_op | source)
XLA Modules:
  0.0 115.0 jit_solution(2382742495407956088)
XLA Ops:
  0.6 4.9 %shard_map.131 = bf16[7168,128]{1,0:T(8,128)(2,1)} custom-call(s32[1,128]{1,0:T(1,128)} %tok_ref.1, bf16[512,2048]{1,0:T(8,128)(2,1)} %emb_ref.1, bf16[1,128,2048]{2,1,0:T(8,128)(2,1)} %in_ref.1, bf16[1,128,2048]{2,1,0:T(8,128)(2,1)} %stud_ref.1, bf16[1,128,2048]{2,1,0:T(8,128)(2,1)} %teach_ref.1, bf16[128,2048]{1,0:T(8,128)(2,1)} %ft_ref.1, ...), custom_call_target="tpu_custom_call" | custom-call | tf_op jit(solution)/shard_map/pallas_call | solution.py:155
  5.5 0.0 copy-start
  5.6 0.0 copy-start.1
  5.6 0.0 copy-start.2
  5.6 0.0 copy-start.3
  5.6 0.0 copy-start.4
  5.6 63.1 %all_to_all.10 = bf16[256,7,4,128]{3,2,1,0:T(4,128)(2,1)S(1)} all-to-all(bf16[256,7,4,128]{3,2,1,0:T(4,128)(2,1)} %bitcast.3), channel_id=1, replica_groups=mesh['ctx'=64,'dp'=4] {'dp','ctx'}, dimensions={0} | all-to-all | bytes 3670016 | tf_op jit(solution)/shard_map/all_to_all | solution.py:365
  68.7 0.0 copy-done
  68.7 0.0 copy-done.1
  68.7 0.0 copy-done.2
  68.7 0.0 copy-done.3
  68.7 0.0 copy-done.4
  68.8 7.3 %shard_map.132 = bf16[256,16,128]{2,1,0:T(8,128)(2,1)S(1)} custom-call(bf16[7168,128]{1,0:T(8,128)(2,1)S(1)} %bitcast.2, bf16[1024,512]{1,0:T(8,128)(2,1)S(1)} %copy-done.1, bf16[512,1024]{1,0:T(8,128)(2,1)S(1)} %copy-done, f32[2,512,128]{2,1,0:T(8,128)S(1)} %copy-done.2, bf16[256,256]{1,0:T(8,128)(2,1)S(1)} %copy-done.4, bf16[256,256]{1,0:T(8,128)(2,1)S(1)} %copy-done.3), custom_call_target="tpu_custom_call" | custom-call | tf_op jit(solution)/shard_map/pallas_call | solution.py:316
  76.1 36.8 %all_to_all.11.in_ref = bf16[256,16,128]{2,1,0:T(8,128)(2,1)S(1)} all-to-all(bf16[256,16,128]{2,1,0:T(8,128)(2,1)S(1)} %shard_map.132), channel_id=1, replica_groups=mesh['ctx'=64,'dp'=4] {'dp','ctx'}, dimensions={0} | all-to-all | bytes 2097152 | tf_op jit(solution)/shard_map/all_to_all | solution.py:365
  112.9 2.1 %shard_map.133 = (bf16[1,128,2048]{2,1,0:T(8,128)(2,1)}, f32[128,2048]{1,0:T(8,128)}) custom-call(bf16[256,16,128]{2,1,0:T(8,128)(2,1)S(1)} %all_to_all.11.in_ref), custom_call_target="tpu_custom_call" | custom-call | tf_op jit(solution)/shard_map/pallas_call | solution.py:345
Async XLA Ops:
  5.5 63.2 %copy-start = (bf16[512,1024]{1,0:T(8,128)(2,1)S(1)}, bf16[512,1024]{1,0:T(8,128)(2,1)}, u32[]{:S(2)}) copy-start(bf16[512,1024]{1,0:T(8,128)(2,1)} %constant.11.clone.t1i_ref) | copy-start | bytes 3145732
  5.6 63.2 %copy-start.1 = (bf16[1024,512]{1,0:T(8,128)(2,1)S(1)}, bf16[1024,512]{1,0:T(8,128)(2,1)}, u32[]{:S(2)}) copy-start(bf16[1024,512]{1,0:T(8,128)(2,1)} %constant.10.clone.t1_ref) | copy-start | bytes 3145732
  5.6 63.2 %copy-start.2 = (f32[2,512,128]{2,1,0:T(8,128)S(1)}, f32[2,512,128]{2,1,0:T(8,128)}, u32[]{:S(2)}) copy-start(f32[2,512,128]{2,1,0:T(8,128)} %constant.12.clone.turn_ref) | copy-start | bytes 1572868
  5.6 63.2 %copy-start.3 = (bf16[256,256]{1,0:T(8,128)(2,1)S(1)}, bf16[256,256]{1,0:T(8,128)(2,1)}, u32[]{:S(2)}) copy-start(bf16[256,256]{1,0:T(8,128)(2,1)} %constant.14.clone.t2i_ref) | copy-start | bytes 393220
  5.6 63.2 %copy-start.4 = (bf16[256,256]{1,0:T(8,128)(2,1)S(1)}, bf16[256,256]{1,0:T(8,128)(2,1)}, u32[]{:S(2)}) copy-start(bf16[256,256]{1,0:T(8,128)(2,1)} %constant.13.clone.t2_ref) | copy-start | bytes 393220

commit v3 on v2

--- a/solution.py
+++ b/solution.py
@@ -12,8 +12,9 @@
 SUB = 8
 HALF = 4
 MESSAGE = 28
+REPLY = 12
 LANES = 128
-CHUNK = 256
+CHUNK = 512
 MIB = 1 << 20
 
 
@@ -46,18 +47,8 @@
     return jnp.dot(a, b, preferred_element_type=jnp.float32)
 
 
-def dot_nt(a, b):
-    return lax.dot_general(a, b, (((1,), (1,)), ((), ())), preferred_element_type=jnp.float32)
-
-
 def turned(x):
     return x.T.astype(jnp.float32)
-
-
-def unit(size):
-    rows = lax.broadcasted_iota(jnp.int32, (size, size), 0)
-    cols = lax.broadcasted_iota(jnp.int32, (size, size), 1)
-    return (rows == cols).astype(jnp.float32).astype(jnp.bfloat16)
 
 
 def half_turn(x):
@@ -71,7 +62,7 @@
 
 def pack_kernel(
     width, tok_ref, emb_ref, in_ref, stud_ref, teach_ref, ft_ref, fs_ref, out_ref,
-    emb_buf, data_buf, sems,
+    emb_buf, data_buf, out_buf, sems, out_sems,
 ):
     vocab, channels = emb_ref.shape
     toks = tok_ref.shape[1]
@@ -123,7 +114,7 @@
         place = pl.ds(chunk * pairs * 2 * MESSAGE, pairs * 2 * MESSAGE)
 
         def store(tiles):
-            out_ref[place, :] = (
+            out_buf[place, :] = (
                 jnp.stack(tiles, axis=1).reshape(pairs * 2 * MESSAGE, toks).astype(jnp.bfloat16)
             )
 
@@ -145,6 +136,16 @@
                 halves(tap_upper, mix), halves(mix, stud), halves(stud, teach),
                 halves(teach, tap_lower),
             ] + [x[:, 1] for x in parts[:3]])
+
+        pltpu.make_async_copy(
+            out_buf.at[place, :], out_ref.at[place, :], out_sems.at[chunk]
+        ).start()
+
+    for chunk in range(chunks):
+        place = pl.ds(chunk * pairs * 2 * MESSAGE, pairs * 2 * MESSAGE)
+        pltpu.make_async_copy(
+            out_buf.at[place, :], out_ref.at[place, :], out_sems.at[chunk]
+        ).wait()
 
 
 def pack(token_ids, embedding, in_gate, teacher_gate, student_gate, teacher_filter, student_filter):
@@ -155,12 +156,14 @@
     return pl.pallas_call(
         functools.partial(pack_kernel, width),
         in_specs=[pl.BlockSpec(memory_space=pltpu.VMEM)] + [here] * 6,
-        out_specs=pl.BlockSpec(memory_space=pltpu.VMEM),
+        out_specs=here,
         out_shape=jax.ShapeDtypeStruct((channels // SUB * MESSAGE, toks), jnp.bfloat16),
         scratch_shapes=[
             pltpu.VMEM((vocab, channels), jnp.bfloat16),
             pltpu.VMEM((4, toks, channels), jnp.bfloat16),
+            pltpu.VMEM((channels // SUB * MESSAGE, toks), jnp.bfloat16),
             pltpu.SemaphoreType.DMA((channels // width, 5)),
+            pltpu.SemaphoreType.DMA((channels // width,)),
         ],
         compiler_params=pltpu.CompilerParams(vmem_limit_bytes=60 * MIB),
     )(token_ids, embedding, in_gate, student_gate, teacher_gate, teacher_filter, student_filter)
@@ -297,12 +300,17 @@
     def finish(chunk, carry):
         rows = pl.ds(pl.multiple_of(chunk * CHUNK, CHUNK), CHUNK)
         lags = dot(t1i_ref[rows, :], lag_ref[...])
-        lags = ((lags[:, :toks] + lags[:, toks:]) * scale).reshape(per, SUB, toks)
+        lags = ((lags[:, :toks] + lags[:, toks:]) * scale).reshape(per // 2, 2, SUB, toks)
+        turned_lags = half_turn(lags.reshape(per, SUB, toks)).reshape(lags.shape)
+        middle = (
+            halves(lags[:, 0], turned_lags[:, 1]),
+            halves(turned_lags[:, 0], lags[:, 1]),
+        )
         for d in range(seqs):
-            stud = stud_ref[rows, lanes(d)].reshape(per, SUB, toks)
-            out_ref[pl.ds(d * blocks + chunk * per, per)] = jnp.concatenate(
-                [stud, lags], axis=1
-            ).astype(bf)
+            stud = stud_ref[rows, lanes(d)].reshape(per // 2, 2, SUB, toks)
+            tiles = jnp.stack([stud[:, 0], middle[d % 2], stud[:, 1]], axis=1)
+            place = pl.multiple_of((d * blocks + chunk * per) * REPLY, per * REPLY)
+            out_ref[pl.ds(place, per * REPLY), :] = tiles.reshape(per * REPLY, toks).astype(bf)
         return carry
 
     lax.fori_loop(0, chunks, finish, 0)
@@ -315,7 +323,7 @@
     bf, f32 = jnp.bfloat16, jnp.float32
     return pl.pallas_call(
         functools.partial(filter_kernel, seqs, blocks, scale),
-        out_shape=jax.ShapeDtypeStruct((seqs * blocks, 2 * SUB, toks), bf),
+        out_shape=jax.ShapeDtypeStruct((seqs * blocks * REPLY, toks), bf),
         scratch_shapes=[
             pltpu.VMEM((full, (seqs + 2) * toks), bf),
             pltpu.VMEM((seqs, full, 2 * toks), f32),
@@ -328,24 +336,47 @@
     )(data, *tables(blocks, toks))
 
 
-def unpack_kernel(in_ref, stud_ref, lag_ref):
-    count, _, toks = in_ref.shape
-    data = in_ref[...].astype(jnp.float32)
-    eye = unit(toks)
-    stud = data[:, :SUB, :].reshape(count * SUB, toks).astype(jnp.bfloat16)
-    lags = data[:, SUB:, :].reshape(count * SUB, toks).astype(jnp.bfloat16)
-    stud_ref[0] = dot_nt(eye, stud).astype(jnp.bfloat16)
-    lag_ref[...] = dot_nt(eye, lags)
-
-
-def unpack(data):
-    senders, rows, toks = data.shape
-    channels = senders * SUB
-    width = 512
+def unpack_kernel(mine_ref, other_ref, stud_ref, lag_ref):
+    rows, toks = mine_ref.shape
+    pairs = rows // (2 * REPLY)
+    even = lax.rem(lax.axis_index("ctx"), 2) == 0
+    lead = lax.rem(lax.axis_index("dp"), 2) == 0
+
+    def tiles(ref):
+        data = ref[...].astype(jnp.float32).reshape(pairs, 3, SUB, toks)
+        return data[:, 0], data[:, 1], data[:, 2]
+
+    def channels(upper, lower):
+        both = jnp.stack([upper, lower], axis=1).reshape(pairs * 2 * SUB, toks)
+        return both.astype(jnp.bfloat16).T
+
+    first, middle, last = tiles(mine_ref)
+    crossed = half_turn(middle)
+    upper = jnp.where(even, first, halves(half_turn(first), crossed))
+    lower = jnp.where(even, halves(crossed, half_turn(last)), last)
+    stud_ref[0] = channels(upper, lower)
+
+    def taps(first, middle, last):
+        return jnp.where(even, halves(middle, last), halves(first, middle))
+
+    mine = taps(first, middle, last)
+    other = taps(*tiles(other_ref))
+    upper = jnp.where(lead, mine, other)
+    lower = jnp.where(lead, other, mine)
+    lag_ref[...] = channels(
+        halves(upper, half_turn(lower)), halves(half_turn(upper), lower)
+    ).astype(jnp.float32)
+
+
+def unpack(mine, other):
+    rows, toks = mine.shape
+    channels = rows // REPLY * SUB
+    width = 1024
+    message = pl.BlockSpec((width // SUB * REPLY, toks), lambda g: (g, 0))
     return pl.pallas_call(
         unpack_kernel,
         grid=(channels // width,),
-        in_specs=[pl.BlockSpec((width // SUB, rows, toks), lambda g: (g, 0, 0))],
+        in_specs=[message, message],
         out_specs=(
             pl.BlockSpec((1, toks, width), lambda g: (0, 0, g)),
             pl.BlockSpec((toks, width), lambda g: (0, g)),
@@ -355,19 +386,20 @@
             jax.ShapeDtypeStruct((toks, channels), jnp.float32),
         ),
         compiler_params=pltpu.CompilerParams(vmem_limit_bytes=32 * MIB),
-    )(data)
+    )(mine, other)
 
 
 def body(*args):
     seqs, blocks = lax.axis_size("dp"), lax.axis_size("ctx")
 
     def exchange(x):
-        return lax.all_to_all(x, ("dp", "ctx"), split_axis=0, concat_axis=0, tiled=True)
-
-    sent = pack(*args)
-    toks = sent.shape[1]
-    got = exchange(sent.reshape(seqs * blocks, MESSAGE // HALF, HALF, toks))
-    return unpack(exchange(filters(got.reshape(sent.shape), seqs, blocks)))
+        cut = x.reshape(seqs * blocks, -1, HALF, x.shape[1])
+        got = lax.all_to_all(cut, ("dp", "ctx"), split_axis=0, concat_axis=0, tiled=True)
+        return got.reshape(x.shape)
+
+    got = exchange(filters(exchange(pack(*args)), seqs, blocks))
+    partner = [(d, d + 1 - 2 * (d % 2)) for d in range(seqs)]
+    return unpack(got, lax.ppermute(got, "dp", partner))
 
 
 def solution(mesh):

time: 115 us -> 111 us (0.965)
  blocking collectives: 99.9 us -> 94.3 us
  Pallas kernels: 14.3 us -> 12 us
  waiting for transfers between devices: 0 us -> 1.91 us
  starting transfers between devices: 0 us -> 1.46 us
    all_to_all x2, blocking collectives: 99.9 us -> 94.3 us  [exchange(): lax.all_to_all(cut, ('dp', 'ctx'), split_axis=0, concat_axis=0, tiled=True)]
    ppermute x0 -> x1, waiting for transfers between devices: none -> 1.91 us  [body(): return unpack(got, lax.ppermute(got, 'dp', partner))]
    ppermute x0 -> x1, starting transfers between devices: none -> 1.46 us  [body(): return unpack(got, lax.ppermute(got, 'dp', partner))]
  transfers between devices with their start and end apart: 0 -> 1, of which waited for: 0 -> 1; matrix products, arithmetic and copies ran while one was open for 0% -> 0% of each run, Pallas kernels for 0% -> 0%
where the time goes in v3:
time: 111 us; the launch traced here: 110 us
  blocking collectives  94.3 us (85%)
  Pallas kernels  12 us (11%)
  waiting for transfers between devices  1.91 us (2%)
  starting transfers between devices  1.46 us (1%)
    all_to_all x2, blocking collectives, exchange(): lax.all_to_all(cut, ('dp', 'ctx'), split_axis=0, concat_axis=0, tiled=True)  94.3 us
    pallas_call x1, Pallas kernels, filters(): pl.pallas_call(functools.partial(filter_kernel, seqs, blocks, scale), out...  6.17 us
    pallas_call x1, Pallas kernels, pack(): pl.pallas_call(functools.partial(pack_kernel, width), in_specs=[pl.BlockS...  4.45 us
  transfers between devices with their start and end apart: 1, of which 1 were waited for; matrix products, arithmetic and copies ran while one was open for 0% of the time, Pallas kernels for 0%

profile of v3, /device:TPU:1, one launch (start us, length us, event | category | flops | bytes accessed | tf_op | source)
XLA Modules:
  0.0 110.5 jit_solution(15338295435392867129)
XLA Ops:
  0.6 4.5 %shard_map.131 = bf16[7168,128]{1,0:T(8,128)(2,1)} custom-call(s32[1,128]{1,0:T(1,128)} %tok_ref.1, bf16[512,2048]{1,0:T(8,128)(2,1)} %emb_ref.1, bf16[1,128,2048]{2,1,0:T(8,128)(2,1)} %in_ref.1, bf16[1,128,2048]{2,1,0:T(8,128)(2,1)} %stud_ref.1, bf16[1,128,2048]{2,1,0:T(8,128)(2,1)} %teach_ref.1, bf16[128,2048]{1,0:T(8,128)(2,1)} %ft_ref.1, ...), custom_call_target="tpu_custom_call" | custom-call | tf_op jit(solution)/shard_map/pallas_call | solution.py:156
  5.1 0.0 copy-start
  5.1 0.0 copy-start.1
  5.1 0.0 copy-start.2
  5.1 0.0 copy-start.3
  5.1 0.0 copy-start.4
  5.2 63.1 %all_to_all.10 = bf16[256,7,4,128]{3,2,1,0:T(4,128)(2,1)S(1)} all-to-all(bf16[256,7,4,128]{3,2,1,0:T(4,128)(2,1)} %bitcast.8), channel_id=1, replica_groups=mesh['ctx'=64,'dp'=4] {'dp','ctx'}, dimensions={0} | all-to-all | bytes 3670016 | tf_op jit(solution)/shard_map/all_to_all | solution.py:397
  68.3 0.0 copy-done
  68.3 0.0 copy-done.1
  68.3 0.0 copy-done.2
  68.3 0.0 copy-done.3
  68.3 0.0 copy-done.4
  68.3 6.2 %shard_map.132 = bf16[3072,128]{1,0:T(8,128)(2,1)S(1)} custom-call(bf16[7168,128]{1,0:T(8,128)(2,1)S(1)} %bitcast.4, bf16[1024,512]{1,0:T(8,128)(2,1)S(1)} %copy-done.1, bf16[512,1024]{1,0:T(8,128)(2,1)S(1)} %copy-done, f32[2,512,128]{2,1,0:T(8,128)S(1)} %copy-done.2, bf16[256,256]{1,0:T(8,128)(2,1)S(1)} %copy-done.4, bf16[256,256]{1,0:T(8,128)(2,1)S(1)} %copy-done.3), custom_call_target="tpu_custom_call" | custom-call | tf_op jit(solution)/shard_map/pallas_call | solution.py:324
  74.5 31.2 %all_to_all.11 = bf16[256,3,4,128]{3,2,1,0:T(4,128)(2,1)S(1)} all-to-all(bf16[256,3,4,128]{3,2,1,0:T(4,128)(2,1)S(1)} %bitcast.7), channel_id=1, replica_groups=mesh['ctx'=64,'dp'=4] {'dp','ctx'}, dimensions={0} | all-to-all | bytes 1572864 | tf_op jit(solution)/shard_map/all_to_all | solution.py:397
  105.7 1.5 %collective-permute-start = (bf16[3072,128]{1,0:T(8,128)(2,1)S(1)}, bf16[3072,128]{1,0:T(8,128)(2,1)S(1)}, u32[]{:S(2)}, u32[]{:S(2)}) collective-permute-start(bf16[3072,128]{1,0:T(8,128)(2,1)S(1)} %bitcast.5), channel_id=1, source_target_pairs={{0,1},{1,0},{2,3},{3,2},{4,5},{5,4},{6,7},{7,6},{8,9},{9,8},{10,11... | collective-permute-start | bytes 2359304 | tf_op jit(solution)/shard_map/ppermute | solution.py:402
  107.1 1.9 %collective-permute-done.other_ref = bf16[3072,128]{1,0:T(8,128)(2,1)S(1)} collective-permute-done((bf16[3072,128]{1,0:T(8,128)(2,1)S(1)}, bf16[3072,128]{1,0:T(8,128)(2,1)S(1)}, u32[]{:S(2)}, u32[]{:S(2)}) %collective-permute-start) | collective-permute-done | bytes 786464 | tf_op jit(solution)/shard_map/ppermute | solution.py:402
  109.0 1.4 %shard_map.133 = (bf16[1,128,2048]{2,1,0:T(8,128)(2,1)}, f32[128,2048]{1,0:T(8,128)}) custom-call(bf16[3072,128]{1,0:T(8,128)(2,1)S(1)} %bitcast.6, bf16[3072,128]{1,0:T(8,128)(2,1)S(1)} %collective-permute-done.other_ref), custom_call_target="tpu_custom_call" | custom-call | tf_op jit(solution)/shard_map/pallas_call | solution.py:376
Async XLA Ops:
  5.1 63.2 %copy-start = (bf16[512,1024]{1,0:T(8,128)(2,1)S(1)}, bf16[512,1024]{1,0:T(8,128)(2,1)}, u32[]{:S(2)}) copy-start(bf16[512,1024]{1,0:T(8,128)(2,1)} %constant.11.clone.t1i_ref) | copy-start | bytes 3145732
  5.1 63.2 %copy-start.1 = (bf16[1024,512]{1,0:T(8,128)(2,1)S(1)}, bf16[1024,512]{1,0:T(8,128)(2,1)}, u32[]{:S(2)}) copy-start(bf16[1024,512]{1,0:T(8,128)(2,1)} %constant.10.clone.t1_ref) | copy-start | bytes 3145732
  5.1 63.2 %copy-start.2 = (f32[2,512,128]{2,1,0:T(8,128)S(1)}, f32[2,512,128]{2,1,0:T(8,128)}, u32[]{:S(2)}) copy-start(f32[2,512,128]{2,1,0:T(8,128)} %constant.12.clone.turn_ref) | copy-start | bytes 1572868
  5.1 63.2 %copy-start.3 = (bf16[256,256]{1,0:T(8,128)(2,1)S(1)}, bf16[256,256]{1,0:T(8,128)(2,1)}, u32[]{:S(2)}) copy-start(bf16[256,256]{1,0:T(8,128)(2,1)} %constant.14.clone.t2i_ref) | copy-start | bytes 393220
  5.1 63.2 %copy-start.4 = (bf16[256,256]{1,0:T(8,128)(2,1)S(1)}, bf16[256,256]{1,0:T(8,128)(2,1)}, u32[]{:S(2)}) copy-start(bf16[256,256]{1,0:T(8,128)(2,1)} %constant.13.clone.t2_ref) | copy-start | bytes 393220
  105.7 3.4 %collective-permute-start = (bf16[3072,128]{1,0:T(8,128)(2,1)S(1)}, bf16[3072,128]{1,0:T(8,128)(2,1)S(1)}, u32[]{:S(2)}, u32[]{:S(2)}) collective-permute-start(bf16[3072,128]{1,0:T(8,128)(2,1)S(1)} %bitcast.5), channel_id=1, source_target_pairs={{0,1},{1,0},{2,3},{3,2},{4,5},{5,4},{6,7},{7,6},{8,9},{9,8},{10,11... | collective-permute-start | bytes 2359304 | tf_op jit(solution)/shard_map/ppermute | solution.py:402

commit v4 on v3

v4 whole, which is shorter than its diff:
```python
import functools

import jax
import jax.numpy as jnp
import numpy as np
from jax import lax
from jax.experimental import pallas as pl
from jax.experimental.pallas import tpu as pltpu
from jax.sharding import PartitionSpec as P

SUB = 8
HALF = 4
MESSAGE = 28
REPLY = 12
MIB = 1 << 20


def tables(blocks, inner):
    span = 2 * blocks * inner
    freq = np.arange(blocks, dtype=np.float64) + 0.5
    pos = np.arange(blocks, dtype=np.float64)
    lane = np.arange(inner, dtype=np.float64)
    angle = 2.0 * np.pi * ((freq[:, None] * pos[None, :]) % (2 * blocks)) / (2 * blocks)
    both = np.stack([np.cos(angle), -np.sin(angle)])
    spread = np.einsum("rka,im->rkiam", both, np.eye(HALF))
    swapped = spread.reshape(2, blocks, HALF, blocks // 2, 2, HALF)[:, :, :, :, ::-1]
    shape = (2 * blocks * HALF, blocks * HALF)
    first = np.stack([spread.reshape(shape), swapped.reshape(shape)])
    turn = 2.0 * np.pi * (freq[:, None] * lane[None, :]) / span
    turn = np.repeat(np.stack([np.cos(turn), np.sin(turn)]), HALF, axis=1)
    turn = np.concatenate([turn, turn], axis=1)
    angle = 2.0 * np.pi * ((lane[:, None] * lane[None, :]) % inner) / inner
    cosines, sines = np.cos(angle), np.sin(angle)
    second = np.block([[cosines, -sines], [sines, cosines]])
    bf = jnp.bfloat16
    return (
        jnp.asarray(first, bf),
        jnp.asarray(first.transpose(0, 2, 1) * (2.0 / span), bf),
        jnp.asarray(turn, jnp.float32),
        jnp.asarray(second, bf),
        jnp.asarray(second.T, bf),
    )


def dot(a, b):
    return jnp.dot(a, b, preferred_element_type=jnp.float32)


def turned(x):
    return x.T.astype(jnp.float32)


def half_turn(x):
    return jnp.concatenate([x[:, HALF:], x[:, :HALF]], axis=1)


def halves(upper, lower):
    rows = lax.broadcasted_iota(jnp.int32, upper.shape, 1)
    return jnp.where(rows < HALF, upper, lower)


def pack_kernel(
    width, tok_ref, emb_ref, in_ref, stud_ref, teach_ref, ft_ref, fs_ref, out_ref,
    emb_buf, data_buf, out_buf, sems, out_sems,
):
    vocab, channels = emb_ref.shape
    toks = tok_ref.shape[1]
    chunks = channels // width
    pairs = width // (2 * SUB)
    dp = lax.axis_index("dp")
    teacher = dp < lax.axis_size("dp") // 2
    lead = lax.rem(dp, 2) == 0
    even = lax.rem(lax.axis_index("ctx"), 2) == 0

    def copies(chunk, taps):
        cols = pl.ds(chunk * width, width)
        sources = (
            (emb_ref.at[:, cols], emb_buf.at[:, cols]),
            (in_ref.at[0, :, cols], data_buf.at[0, :, cols]),
            (stud_ref.at[0, :, cols], data_buf.at[1, :, cols]),
            (teach_ref.at[0, :, cols], data_buf.at[2, :, cols]),
            (taps.at[:, cols], data_buf.at[3, :, cols]),
        )
        return [
            (src, dst, sems.at[chunk, n]) for n, (src, dst) in enumerate(sources)
        ]

    for chunk in range(chunks):
        for copy in copies(chunk, ft_ref)[:4]:
            pltpu.make_async_copy(*copy).start()

        @pl.when(teacher)
        def _():
            pltpu.make_async_copy(*copies(chunk, ft_ref)[4]).start()

        @pl.when(jnp.logical_not(teacher))
        def _():
            pltpu.make_async_copy(*copies(chunk, fs_ref)[4]).start()

    rows = lax.broadcasted_iota(jnp.int32, (vocab, toks), 0)
    one_hot = (rows == tok_ref[...]).astype(jnp.float32).T.astype(jnp.bfloat16)

    for chunk in range(chunks):
        for copy in copies(chunk, ft_ref):
            pltpu.make_async_copy(*copy).wait()
        cols = pl.ds(chunk * width, width)
        values = dot(one_hot, emb_buf[:, cols])
        mixed = (data_buf[0, :, cols].astype(jnp.float32) * values).astype(jnp.bfloat16)
        parts = [
            turned(x).reshape(pairs, 2, SUB, toks)
            for x in (mixed, data_buf[1, :, cols], data_buf[2, :, cols], data_buf[3, :, cols])
        ]
        place = pl.ds(chunk * pairs * 2 * MESSAGE, pairs * 2 * MESSAGE)

        def store(tiles):
            out_buf[place, :] = (
                jnp.stack(tiles, axis=1).reshape(pairs * 2 * MESSAGE, toks).astype(jnp.bfloat16)
            )

        tap_upper = jnp.where(lead, parts[3][:, 0], half_turn(parts[3][:, 0]))
        tap_lower = jnp.where(lead, half_turn(parts[3][:, 1]), parts[3][:, 1])

        @pl.when(even)
        def _():
            mix, stud, teach = [half_turn(x[:, 1]) for x in parts[:3]]
            store([x[:, 0] for x in parts[:3]] + [
                halves(tap_upper, mix), halves(mix, stud), halves(stud, teach),
                halves(teach, tap_lower),
            ])

        @pl.when(jnp.logical_not(even))
        def _():
            mix, stud, teach = [x[:, 0] for x in parts[:3]]
            store([
                halves(tap_upper, mix), halves(mix, stud), halves(stud, teach),
                halves(teach, tap_lower),
            ] + [half_turn(x[:, 1]) for x in parts[:3]])

        pltpu.make_async_copy(
            out_buf.at[place, :], out_ref.at[place, :], out_sems.at[chunk]
        ).start()

    for chunk in range(chunks):
        place = pl.ds(chunk * pairs * 2 * MESSAGE, pairs * 2 * MESSAGE)
        pltpu.make_async_copy(
            out_buf.at[place, :], out_ref.at[place, :], out_sems.at[chunk]
        ).wait()


def pack(token_ids, embedding, in_gate, teacher_gate, student_gate, teacher_filter, student_filter):
    vocab, channels = embedding.shape
    toks = token_ids.shape[1]
    width = 512
    here = pl.BlockSpec(memory_space=pl.ANY)
    return pl.pallas_call(
        functools.partial(pack_kernel, width),
        in_specs=[pl.BlockSpec(memory_space=pltpu.VMEM)] + [here] * 6,
        out_specs=here,
        out_shape=jax.ShapeDtypeStruct((channels // SUB * MESSAGE, toks), jnp.bfloat16),
        scratch_shapes=[
            pltpu.VMEM((vocab, channels), jnp.bfloat16),
            pltpu.VMEM((4, toks, channels), jnp.bfloat16),
            pltpu.VMEM((channels // SUB * MESSAGE, toks), jnp.bfloat16),
            pltpu.SemaphoreType.DMA((channels // width, 5)),
            pltpu.SemaphoreType.DMA((channels // width,)),
        ],
        compiler_params=pltpu.CompilerParams(vmem_limit_bytes=60 * MIB),
    )(token_ids, embedding, in_gate, student_gate, teacher_gate, teacher_filter, student_filter)


def filter_kernel(
    seqs, blocks, scale, in_ref, t1_ref, t1i_ref, turn_ref, t2_ref, t2i_ref, out_ref,
    x_ref, spec_ref, wave_ref, grad_ref, stud_ref, lag_ref,
):
    bf, f32 = jnp.bfloat16, jnp.float32
    toks = in_ref.shape[1]
    full = blocks * SUB
    half = full // 2
    pairs = blocks // 2
    cosines, sines = turn_ref[0], turn_ref[1]

    def received(seq):
        size = blocks * MESSAGE
        data = in_ref[pl.ds(seq * size, size), :].astype(f32)
        return data.reshape(pairs, 2 * MESSAGE // SUB, SUB, toks)

    def sets(data, part):
        even, odd = data[:, part], data[:, part + HALF]
        return jnp.concatenate(
            [halves(even, odd).reshape(half, toks), halves(odd, even).reshape(half, toks)], axis=0
        )

    def lanes(n):
        return pl.ds(n * toks, toks)

    def columns(x, n):
        return x[:, n * toks:(n + 1) * toks]

    for d in range(seqs):
        data = received(d)
        x_ref[:, lanes(d)] = sets(data, 0).astype(bf)
        rows = pl.ds((d % 2) * half, half)
        taps = half_turn(data[:, HALF - 1]) if d % 2 else data[:, HALF - 1]
        x_ref[rows, lanes(seqs + d // 2)] = taps.reshape(half, toks).astype(bf)

    def forward(ref, count):
        outs = [dot(t1_ref[n], ref[pl.ds(n * half, half), :]) for n in range(2)]
        parts = []
        for n in range(count):
            re = jnp.concatenate([columns(out[:half], n) for out in outs], axis=0)
            im = jnp.concatenate([columns(out[half:], n) for out in outs], axis=0)
            parts.append(
                jnp.concatenate([re * cosines + im * sines, im * cosines - re * sines], axis=1)
                .astype(bf)
            )
        return dot(jnp.concatenate(parts, axis=0), t2_ref[...])

    def back(prod):
        re, im = columns(prod, 0), columns(prod, 1)
        return re * cosines - im * sines, im * cosines + re * sines

    def keep(ref, n, re, im):
        ref[pl.ds(0, half), lanes(n)] = re[:half].astype(bf)
        ref[pl.ds(half, half), lanes(n)] = im[:half].astype(bf)
        ref[pl.ds(full, half), lanes(n)] = re[half:].astype(bf)
        ref[pl.ds(full + half, half), lanes(n)] = im[half:].astype(bf)

    def last(ref):
        return [dot(t1i_ref[n], ref[pl.ds(n * full, full), :]) for n in range(2)]

    spec = forward(x_ref, seqs + 2)
    spec_ref[...] = spec[:seqs * full]
    for f in range(2):
        taps = spec[(seqs + f) * full:(seqs + f + 1) * full]
        tr, ti = columns(taps, 0), columns(taps, 1)
        prods = []
        for d in range(seqs):
            ur = columns(spec[d * full:(d + 1) * full], 0)
            ui = columns(spec[d * full:(d + 1) * full], 1)
            prods.append(
                jnp.concatenate([ur * tr - ui * ti, ur * ti + ui * tr], axis=1).astype(bf)
            )
        waves = dot(jnp.concatenate(prods, axis=0), t2i_ref[...])
        for d in range(seqs):
            keep(wave_ref, f * seqs + d, *back(waves[d * full:(d + 1) * full]))

    conv = jnp.concatenate(last(wave_ref), axis=0).astype(bf).astype(f32)
    for d in range(seqs):
        data = received(d)
        gate_s = sets(data, 1)
        stud = gate_s * columns(conv, seqs + d)
        stud_ref[:, lanes(d)] = stud
        grad = gate_s * (stud - sets(data, 2) * columns(conv, d))
        grad_ref[:, lanes(d)] = grad.astype(bf)

    spec = forward(grad_ref, seqs)
    sum_re = jnp.zeros((full, toks), f32)
    sum_im = jnp.zeros((full, toks), f32)
    for d in range(seqs):
        gr = columns(spec[d * full:(d + 1) * full], 0)
        gi = columns(spec[d * full:(d + 1) * full], 1)
        ur = spec_ref[pl.ds(d * full, full), lanes(0)]
        ui = spec_ref[pl.ds(d * full, full), lanes(1)]
        sum_re += gr * ur + gi * ui
        sum_im += gi * ur - gr * ui
    total = jnp.concatenate([sum_re, sum_im], axis=1)
    high = total.astype(bf)
    low = (total - high.astype(f32)).astype(bf)
    waves = dot(jnp.concatenate([high, low], axis=0), t2i_ref[...])
    re, im = back(waves[:full] + waves[full:])
    high_re, high_im = [x.astype(bf).astype(f32) for x in (re, im)]
    keep(lag_ref, 0, high_re, high_im)
    keep(lag_ref, 1, re - high_re, im - high_im)
    lags = [
        ((columns(x, 0) + columns(x, 1)) * scale).reshape(pairs, SUB, toks) for x in last(lag_ref)
    ]
    middle = (lags[0], half_turn(lags[1]))
    for d in range(seqs):
        first = stud_ref[pl.ds(0, half), lanes(d)].reshape(pairs, SUB, toks)
        second = stud_ref[pl.ds(half, half), lanes(d)].reshape(pairs, SUB, toks)
        tiles = jnp.stack([halves(first, second), middle[d % 2], halves(second, first)], axis=1)
        size = blocks * REPLY
        out_ref[pl.ds(d * size, size), :] = tiles.reshape(size, toks).astype(bf)


def filters(data, seqs, blocks):
    toks = data.shape[1]
    full = blocks * SUB
    scale = float(seqs * blocks * toks) ** -0.5
    bf, f32 = jnp.bfloat16, jnp.float32
    return pl.pallas_call(
        functools.partial(filter_kernel, seqs, blocks, scale),
        out_shape=jax.ShapeDtypeStruct((seqs * blocks * REPLY, toks), bf),
        scratch_shapes=[
            pltpu.VMEM((full, (seqs + 2) * toks), bf),
            pltpu.VMEM((seqs * full, 2 * toks), f32),
            pltpu.VMEM((2 * full, 2 * seqs * toks), bf),
            pltpu.VMEM((full, seqs * toks), bf),
            pltpu.VMEM((full, seqs * toks), f32),
            pltpu.VMEM((2 * full, 2 * toks), bf),
        ],
        compiler_params=pltpu.CompilerParams(vmem_limit_bytes=48 * MIB),
    )(data, *tables(blocks, toks))


def tiles(ref):
    rows, toks = ref.shape
    data = ref[...].astype(jnp.float32).reshape(rows // (3 * SUB), 3, SUB, toks)
    return data[:, 0], data[:, 1], data[:, 2]


def channels(upper, lower):
    pairs, _, toks = upper.shape
    both = jnp.stack([upper, lower], axis=1).reshape(pairs * 2 * SUB, toks)
    return both.astype(jnp.bfloat16).T


def student_kernel(in_ref, out_ref):
    even = lax.rem(lax.axis_index("ctx"), 2) == 0
    first, middle, last = tiles(in_ref)
    turned_last = half_turn(last)
    upper = jnp.where(even, first, halves(middle, first))
    lower = jnp.where(even, halves(half_turn(middle), turned_last), turned_last)
    out_ref[0] = channels(upper, lower)


def lags_kernel(mine_ref, other_ref, out_ref):
    even = lax.rem(lax.axis_index("ctx"), 2) == 0
    lead = lax.rem(lax.axis_index("dp"), 2) == 0

    def taps(ref):
        first, middle, last = tiles(ref)
        return jnp.where(even, halves(middle, last), halves(first, middle))

    mine, other = taps(mine_ref), taps(other_ref)
    upper = jnp.where(lead, mine, other)
    lower = jnp.where(lead, other, mine)
    out_ref[...] = channels(
        halves(upper, half_turn(lower)), halves(half_turn(upper), lower)
    ).astype(jnp.float32)


def unpack(mine, other):
    rows, toks = mine.shape
    count = rows // REPLY * SUB
    width = 1024
    message = pl.BlockSpec((width // SUB * REPLY, toks), lambda g: (g, 0))
    params = pltpu.CompilerParams(vmem_limit_bytes=32 * MIB)
    size = pl.CostEstimate(flops=MIB, bytes_accessed=2 * MIB, transcendentals=0)
    student = pl.pallas_call(
        student_kernel,
        grid=(count // width,),
        in_specs=[message],
        out_specs=pl.BlockSpec((1, toks, width), lambda g: (0, 0, g)),
        out_shape=jax.ShapeDtypeStruct((1, toks, count), jnp.bfloat16),
        compiler_params=params,
        cost_estimate=size,
    )(mine)
    lags = pl.pallas_call(
        lags_kernel,
        grid=(count // width,),
        in_specs=[message, message],
        out_specs=pl.BlockSpec((toks, width), lambda g: (0, g)),
        out_shape=jax.ShapeDtypeStruct((toks, count), jnp.float32),
        compiler_params=params,
        cost_estimate=size,
    )(mine, other)
    return student, lags


def body(*args):
    seqs, blocks = lax.axis_size("dp"), lax.axis_size("ctx")

    def exchange(x):
        cut = x.reshape(seqs * blocks, -1, HALF, x.shape[1])
        got = lax.all_to_all(cut, ("dp", "ctx"), split_axis=0, concat_axis=0, tiled=True)
        return got.reshape(x.shape)

    got = exchange(filters(exchange(pack(*args)), seqs, blocks))
    partner = [(d, d + 1 - 2 * (d % 2)) for d in range(seqs)]
    return unpack(got, lax.ppermute(got, "dp", partner))


def solution(mesh):
    placed = (
        P("dp", "ctx"),
        P(),
        P("dp", "ctx", None),
        P("dp", "ctx", None),
        P("dp", "ctx", None),
        P("ctx", None),
        P("ctx", None),
    )
    return jax.shard_map(
        body,
        mesh=mesh,
        in_specs=placed,
        out_specs=(P("dp", "ctx", None), P("ctx", None)),
        check_vma=False,
    )
```

time: 111 us -> 109 us (0.982)
    pallas_call x1, Pallas kernels: 6.17 us -> 4.8 us  [filters(): pl.pallas_call(functools.partial(filter_kernel, seqs, blocks, scale), out...]
    pallas_call x1 -> x2, Pallas kernels: 1.41 us -> 2.26 us  [the longest x1 1.25 us: unpack(): pl.pallas_call(lags_kernel, grid=(count // width,), in_specs=[message, me...]
  transfers between devices with their start and end apart: 1 -> 1, of which waited for: 1 -> 1; matrix products, arithmetic and copies ran while one was open for 0% -> 0% of each run, Pallas kernels for 0% -> 1%
where the time goes in v4:
time: 109 us
  blocking collectives  94.3 us (87%)
  Pallas kernels  11.5 us (11%)
  starting transfers between devices  1.46 us (1%)
    all_to_all x2, blocking collectives, exchange(): lax.all_to_all(cut, ('dp', 'ctx'), split_axis=0, concat_axis=0, tiled=True)  94.3 us
    pallas_call x1, Pallas kernels, filters(): pl.pallas_call(functools.partial(filter_kernel, seqs, blocks, scale), out...  4.8 us
    pallas_call x1, Pallas kernels, pack(): pl.pallas_call(functools.partial(pack_kernel, width), in_specs=[pl.BlockS...  4.45 us
  transfers between devices with their start and end apart: 1, of which 1 were waited for; matrix products, arithmetic and copies ran while one was open for 0% of the time, Pallas kernels for 1%

profile of v4, /device:TPU:1, one launch (start us, length us, event | category | flops | bytes accessed | tf_op | source)
XLA Modules:
  0.0 108.9 jit_solution(16736894782557964277)
XLA Ops:
  0.6 4.4 %shard_map.131 = bf16[7168,128]{1,0:T(8,128)(2,1)} custom-call(s32[1,128]{1,0:T(1,128)} %tok_ref.1, bf16[512,2048]{1,0:T(8,128)(2,1)} %emb_ref.1, bf16[1,128,2048]{2,1,0:T(8,128)(2,1)} %in_ref.1, bf16[1,128,2048]{2,1,0:T(8,128)(2,1)} %stud_ref.1, bf16[1,128,2048]{2,1,0:T(8,128)(2,1)} %teach_ref.1, bf16[128,2048]{1,0:T(8,128)(2,1)} %ft_ref.1, ...), custom_call_target="tpu_custom_call" | custom-call | tf_op jit(solution)/shard_map/pallas_call | solution.py:155
  5.1 0.0 copy-start
  5.1 0.0 copy-start.1
  5.1 0.0 copy-start.2
  5.1 0.0 copy-start.3
  5.1 0.0 copy-start.4
  5.2 63.1 %all_to_all.10 = bf16[256,7,4,128]{3,2,1,0:T(4,128)(2,1)S(1)} all-to-all(bf16[256,7,4,128]{3,2,1,0:T(4,128)(2,1)} %bitcast.9), channel_id=1, replica_groups=mesh['ctx'=64,'dp'=4] {'dp','ctx'}, dimensions={0} | all-to-all | bytes 3670016 | tf_op jit(solution)/shard_map/all_to_all | solution.py:376
  68.3 0.0 copy-done
  68.3 0.0 copy-done.1
  68.3 0.0 copy-done.2
  68.3 0.0 copy-done.3
  68.3 0.0 copy-done.4
  68.3 4.8 %shard_map.132 = bf16[3072,128]{1,0:T(8,128)(2,1)S(1)} custom-call(bf16[7168,128]{1,0:T(8,128)(2,1)S(1)} %bitcast.4, bf16[2,512,256]{2,1,0:T(8,128)(2,1)S(1)} %copy-done.2, bf16[2,256,512]{2,1,0:T(8,128)(2,1)S(1)} %copy-done.1, f32[2,512,128]{2,1,0:T(8,128)S(1)} %copy-done, bf16[256,256]{1,0:T(8,128)(2,1)S(1)} %copy-done.4, bf16[256,256]{1,0:T(8,128)(2,1)S(1)} %copy-done.3), custom_call_target="tpu_custom_call" | custom-call | tf_op jit(solution)/shard_map/pallas_call | solution.py:291
  73.1 31.2 %all_to_all.11 = bf16[256,3,4,128]{3,2,1,0:T(4,128)(2,1)S(1)} all-to-all(bf16[256,3,4,128]{3,2,1,0:T(4,128)(2,1)S(1)} %bitcast.8), channel_id=1, replica_groups=mesh['ctx'=64,'dp'=4] {'dp','ctx'}, dimensions={0} | all-to-all | bytes 1572864 | tf_op jit(solution)/shard_map/all_to_all | solution.py:376
  104.3 1.5 %collective-permute-start = (bf16[3072,128]{1,0:T(8,128)(2,1)S(1)}, bf16[3072,128]{1,0:T(8,128)(2,1)S(1)}, u32[]{:S(2)}, u32[]{:S(2)}) collective-permute-start(bf16[3072,128]{1,0:T(8,128)(2,1)S(1)} %bitcast.5), channel_id=1, source_target_pairs={{0,1},{1,0},{2,3},{3,2},{4,5},{5,4},{6,7},{7,6},{8,9},{9,8},{10,11... | collective-permute-start | bytes 2359304 | tf_op jit(solution)/shard_map/ppermute | solution.py:381
  105.8 1.0 shard_map.133
  106.8 0.9 collective-permute-done.other_ref
  107.7 1.3 %shard_map.134 = f32[128,2048]{1,0:T(8,128)} custom-call(bf16[3072,128]{1,0:T(8,128)(2,1)S(1)} %bitcast.7, bf16[3072,128]{1,0:T(8,128)(2,1)S(1)} %collective-permute-done.other_ref), custom_call_target="tpu_custom_call" | custom-call | flops 1048576 | bytes 2097152 | tf_op jit(solution)/shard_map/pallas_call | solution.py:359
Async XLA Ops:
  5.1 63.2 %copy-start = (f32[2,512,128]{2,1,0:T(8,128)S(1)}, f32[2,512,128]{2,1,0:T(8,128)}, u32[]{:S(2)}) copy-start(f32[2,512,128]{2,1,0:T(8,128)} %constant.12.clone.turn_ref) | copy-start | bytes 1572868
  5.1 63.2 %copy-start.1 = (bf16[2,256,512]{2,1,0:T(8,128)(2,1)S(1)}, bf16[2,256,512]{2,1,0:T(8,128)(2,1)}, u32[]{:S(2)}) copy-start(bf16[2,256,512]{2,1,0:T(8,128)(2,1)} %constant.11.clone.t1i_ref) | copy-start | bytes 1572868
  5.1 63.2 %copy-start.2 = (bf16[2,512,256]{2,1,0:T(8,128)(2,1)S(1)}, bf16[2,512,256]{2,1,0:T(8,128)(2,1)}, u32[]{:S(2)}) copy-start(bf16[2,512,256]{2,1,0:T(8,128)(2,1)} %constant.10.clone.t1_ref) | copy-start | bytes 1572868
  5.1 63.2 %copy-start.3 = (bf16[256,256]{1,0:T(8,128)(2,1)S(1)}, bf16[256,256]{1,0:T(8,128)(2,1)}, u32[]{:S(2)}) copy-start(bf16[256,256]{1,0:T(8,128)(2,1)} %constant.14.clone.t2i_ref) | copy-start | bytes 393220
  5.1 63.2 %copy-start.4 = (bf16[256,256]{1,0:T(8,128)(2,1)S(1)}, bf16[256,256]{1,0:T(8,128)(2,1)}, u32[]{:S(2)}) copy-start(bf16[256,256]{1,0:T(8,128)(2,1)} %constant.13.clone.t2_ref) | copy-start | bytes 393220
  104.3 3.4 %collective-permute-start = (bf16[3072,128]{1,0:T(8,128)(2,1)S(1)}, bf16[3072,128]{1,0:T(8,128)(2,1)S(1)}, u32[]{:S(2)}, u32[]{:S(2)}) collective-permute-start(bf16[3072,128]{1,0:T(8,128)(2,1)S(1)} %bitcast.5), channel_id=1, source_target_pairs={{0,1},{1,0},{2,3},{3,2},{4,5},{5,4},{6,7},{7,6},{8,9},{9,8},{10,11... | collective-permute-start | bytes 2359304 | tf_op jit(solution)/shard_map/ppermute | solution.py:381

commit v5 on v4

--- a/solution.py
+++ b/solution.py
@@ -60,20 +60,22 @@
 
 
 def pack_kernel(
-    width, tok_ref, emb_ref, in_ref, stud_ref, teach_ref, ft_ref, fs_ref, out_ref,
+    widths, tok_ref, emb_ref, in_ref, stud_ref, teach_ref, ft_ref, fs_ref, out_ref,
     emb_buf, data_buf, out_buf, sems, out_sems,
 ):
     vocab, channels = emb_ref.shape
     toks = tok_ref.shape[1]
-    chunks = channels // width
-    pairs = width // (2 * SUB)
+    chunks = len(widths)
     dp = lax.axis_index("dp")
     teacher = dp < lax.axis_size("dp") // 2
     lead = lax.rem(dp, 2) == 0
     even = lax.rem(lax.axis_index("ctx"), 2) == 0
 
+    def span(chunk):
+        return pl.ds(sum(widths[:chunk]) // SUB * MESSAGE, widths[chunk] // SUB * MESSAGE)
+
     def copies(chunk, taps):
-        cols = pl.ds(chunk * width, width)
+        cols = pl.ds(sum(widths[:chunk]), widths[chunk])
         sources = (
             (emb_ref.at[:, cols], emb_buf.at[:, cols]),
             (in_ref.at[0, :, cols], data_buf.at[0, :, cols]),
@@ -103,14 +105,15 @@
     for chunk in range(chunks):
         for copy in copies(chunk, ft_ref):
             pltpu.make_async_copy(*copy).wait()
-        cols = pl.ds(chunk * width, width)
+        pairs = widths[chunk] // (2 * SUB)
+        cols = pl.ds(sum(widths[:chunk]), widths[chunk])
         values = dot(one_hot, emb_buf[:, cols])
         mixed = (data_buf[0, :, cols].astype(jnp.float32) * values).astype(jnp.bfloat16)
         parts = [
             turned(x).reshape(pairs, 2, SUB, toks)
             for x in (mixed, data_buf[1, :, cols], data_buf[2, :, cols], data_buf[3, :, cols])
         ]
-        place = pl.ds(chunk * pairs * 2 * MESSAGE, pairs * 2 * MESSAGE)
+        place = span(chunk)
 
         def store(tiles):
             out_buf[place, :] = (
@@ -141,7 +144,7 @@
         ).start()
 
     for chunk in range(chunks):
-        place = pl.ds(chunk * pairs * 2 * MESSAGE, pairs * 2 * MESSAGE)
+        place = span(chunk)
         pltpu.make_async_copy(
             out_buf.at[place, :], out_ref.at[place, :], out_sems.at[chunk]
         ).wait()
@@ -150,10 +153,10 @@
 def pack(token_ids, embedding, in_gate, teacher_gate, student_gate, teacher_filter, student_filter):
     vocab, channels = embedding.shape
     toks = token_ids.shape[1]
-    width = 512
+    widths = (512,) * (channels // 512)
     here = pl.BlockSpec(memory_space=pl.ANY)
     return pl.pallas_call(
-        functools.partial(pack_kernel, width),
+        functools.partial(pack_kernel, widths),
         in_specs=[pl.BlockSpec(memory_space=pltpu.VMEM)] + [here] * 6,
         out_specs=here,
         out_shape=jax.ShapeDtypeStruct((channels // SUB * MESSAGE, toks), jnp.bfloat16),
@@ -161,8 +164,8 @@
             pltpu.VMEM((vocab, channels), jnp.bfloat16),
             pltpu.VMEM((4, toks, channels), jnp.bfloat16),
             pltpu.VMEM((channels // SUB * MESSAGE, toks), jnp.bfloat16),
-            pltpu.SemaphoreType.DMA((channels // width, 5)),
-            pltpu.SemaphoreType.DMA((channels // width,)),
+            pltpu.SemaphoreType.DMA((len(widths), 5)),
+            pltpu.SemaphoreType.DMA((len(widths),)),
         ],
         compiler_params=pltpu.CompilerParams(vmem_limit_bytes=60 * MIB),
     )(token_ids, embedding, in_gate, student_gate, teacher_gate, teacher_filter, student_filter)
@@ -324,15 +327,20 @@
     out_ref[0] = channels(upper, lower)
 
 
+def pick_kernel(in_ref, out_ref):
+    even = lax.rem(lax.axis_index("ctx"), 2) == 0
+    first, middle, last = tiles(in_ref)
+    taps = jnp.where(even, halves(middle, last), halves(first, middle))
+    out_ref[...] = taps.reshape(out_ref.shape).astype(jnp.bfloat16)
+
+
 def lags_kernel(mine_ref, other_ref, out_ref):
-    even = lax.rem(lax.axis_index("ctx"), 2) == 0
     lead = lax.rem(lax.axis_index("dp"), 2) == 0
-
-    def taps(ref):
-        first, middle, last = tiles(ref)
-        return jnp.where(even, halves(middle, last), halves(first, middle))
-
-    mine, other = taps(mine_ref), taps(other_ref)
+    rows, toks = mine_ref.shape
+    mine, other = [
+        ref[...].astype(jnp.float32).reshape(rows // SUB, SUB, toks)
+        for ref in (mine_ref, other_ref)
+    ]
     upper = jnp.where(lead, mine, other)
     lower = jnp.where(lead, other, mine)
     out_ref[...] = channels(
@@ -340,13 +348,21 @@
     ).astype(jnp.float32)
 
 
-def unpack(mine, other):
-    rows, toks = mine.shape
+def unpack(got, swap):
+    rows, toks = got.shape
     count = rows // REPLY * SUB
     width = 1024
     message = pl.BlockSpec((width // SUB * REPLY, toks), lambda g: (g, 0))
+    picked = pl.BlockSpec((width // 2, toks), lambda g: (g, 0))
     params = pltpu.CompilerParams(vmem_limit_bytes=32 * MIB)
     size = pl.CostEstimate(flops=MIB, bytes_accessed=2 * MIB, transcendentals=0)
+    mine = pl.pallas_call(
+        pick_kernel,
+        out_shape=jax.ShapeDtypeStruct((count // 2, toks), jnp.bfloat16),
+        compiler_params=params,
+        cost_estimate=size,
+    )(got)
+    other = swap(mine)
     student = pl.pallas_call(
         student_kernel,
         grid=(count // width,),
@@ -355,11 +371,11 @@
         out_shape=jax.ShapeDtypeStruct((1, toks, count), jnp.bfloat16),
         compiler_params=params,
         cost_estimate=size,
-    )(mine)
+    )(got)
     lags = pl.pallas_call(
         lags_kernel,
         grid=(count // width,),
-        in_specs=[message, message],
+        in_specs=[picked, picked],
         out_specs=pl.BlockSpec((toks, width), lambda g: (0, g)),
         out_shape=jax.ShapeDtypeStruct((toks, count), jnp.float32),
         compiler_params=params,
@@ -378,7 +394,7 @@
 
     got = exchange(filters(exchange(pack(*args)), seqs, blocks))
     partner = [(d, d + 1 - 2 * (d % 2)) for d in range(seqs)]
-    return unpack(got, lax.ppermute(got, "dp", partner))
+    return unpack(got, lambda x: lax.ppermute(x, "dp", partner))
 
 
 def solution(mesh):

time: 109 us -> 108 us (level)
    pallas_call x2 -> x3, Pallas kernels: 5.7 us -> 5.68 us  [the longest x1 4.45 us: pack(): pl.pallas_call(functools.partial(pack_kernel, widths), in_specs=[pl.Block...]
where the time goes in v5:
time: 108 us
  blocking collectives  94.3 us (87%)
  Pallas kernels  11.5 us (11%)
  starting transfers between devices  1.54 us (1%)
    all_to_all x2, blocking collectives, exchange(): lax.all_to_all(cut, ('dp', 'ctx'), split_axis=0, concat_axis=0, tiled=True)  94.3 us
    pallas_call x1, Pallas kernels, filters(): pl.pallas_call(functools.partial(filter_kernel, seqs, blocks, scale), out...  4.8 us
    pallas_call x1, Pallas kernels, pack(): pl.pallas_call(functools.partial(pack_kernel, widths), in_specs=[pl.Block...  4.45 us
  transfers between devices with their start and end apart: 1, of which 1 were waited for; matrix products, arithmetic and copies ran while one was open for 0% of the time, Pallas kernels for 1%

profile of v5, /device:TPU:1, one launch (start us, length us, event | category | flops | bytes accessed | tf_op | source)
XLA Modules:
  0.0 108.2 jit_solution(7939887598646999892)
XLA Ops:
  0.6 4.4 %shard_map.131 = bf16[7168,128]{1,0:T(8,128)(2,1)} custom-call(s32[1,128]{1,0:T(1,128)} %tok_ref.1, bf16[512,2048]{1,0:T(8,128)(2,1)} %emb_ref.1, bf16[1,128,2048]{2,1,0:T(8,128)(2,1)} %in_ref.1, bf16[1,128,2048]{2,1,0:T(8,128)(2,1)} %stud_ref.1, bf16[1,128,2048]{2,1,0:T(8,128)(2,1)} %teach_ref.1, bf16[128,2048]{1,0:T(8,128)(2,1)} %ft_ref.1, ...), custom_call_target="tpu_custom_call" | custom-call | tf_op jit(solution)/shard_map/pallas_call | solution.py:158
  5.1 0.0 copy-start
  5.1 0.0 copy-start.1
  5.1 0.0 copy-start.2
  5.1 0.0 copy-start.3
  5.1 0.0 copy-start.4
  5.2 63.1 %all_to_all.10 = bf16[256,7,4,128]{3,2,1,0:T(4,128)(2,1)S(1)} all-to-all(bf16[256,7,4,128]{3,2,1,0:T(4,128)(2,1)} %bitcast.8), channel_id=1, replica_groups=mesh['ctx'=64,'dp'=4] {'dp','ctx'}, dimensions={0} | all-to-all | bytes 3670016 | tf_op jit(solution)/shard_map/all_to_all | solution.py:392
  68.3 0.0 copy-done
  68.3 0.0 copy-done.1
  68.3 0.0 copy-done.2
  68.3 0.0 copy-done.3
  68.3 0.0 copy-done.4
  68.3 4.8 %shard_map.132 = bf16[3072,128]{1,0:T(8,128)(2,1)S(1)} custom-call(bf16[7168,128]{1,0:T(8,128)(2,1)S(1)} %bitcast.4, bf16[2,512,256]{2,1,0:T(8,128)(2,1)S(1)} %copy-done.2, bf16[2,256,512]{2,1,0:T(8,128)(2,1)S(1)} %copy-done.1, f32[2,512,128]{2,1,0:T(8,128)S(1)} %copy-done, bf16[256,256]{1,0:T(8,128)(2,1)S(1)} %copy-done.4, bf16[256,256]{1,0:T(8,128)(2,1)S(1)} %copy-done.3), custom_call_target="tpu_custom_call" | custom-call | tf_op jit(solution)/shard_map/pallas_call | solution.py:294
  73.1 31.2 %all_to_all.11 = bf16[256,3,4,128]{3,2,1,0:T(4,128)(2,1)S(1)} all-to-all(bf16[256,3,4,128]{3,2,1,0:T(4,128)(2,1)S(1)} %bitcast.7), channel_id=1, replica_groups=mesh['ctx'=64,'dp'=4] {'dp','ctx'}, dimensions={0} | all-to-all | bytes 1572864 | tf_op jit(solution)/shard_map/all_to_all | solution.py:392
  104.3 0.1 shard_map.134.mine_ref
  104.4 1.5 %collective-permute-start = (bf16[1024,128]{1,0:T(8,128)(2,1)S(1)}, bf16[1024,128]{1,0:T(8,128)(2,1)S(1)}, u32[]{:S(2)}, u32[]{:S(2)}) collective-permute-start(bf16[1024,128]{1,0:T(8,128)(2,1)S(1)} %shard_map.134.mine_ref), channel_id=1, source_target_pairs={{0,1},{1,0},{2,3},{3,2},{4,5},{5,4},{6,7},{7,6},{8,9},{9,8},{10,11... | collective-permute-start | bytes 786440 | tf_op jit(solution)/shard_map/ppermute | solution.py:397
  106.0 1.0 shard_map.133
  107.0 0.2 collective-permute-done.other_ref
  107.1 1.1 %shard_map.135 = f32[128,2048]{1,0:T(8,128)} custom-call(bf16[1024,128]{1,0:T(8,128)(2,1)S(1)} %shard_map.134.mine_ref, bf16[1024,128]{1,0:T(8,128)(2,1)S(1)} %collective-permute-done.other_ref), custom_call_target="tpu_custom_call" | custom-call | flops 1048576 | bytes 2097152 | tf_op jit(solution)/shard_map/pallas_call | solution.py:375
Async XLA Ops:
  5.1 63.2 %copy-start = (f32[2,512,128]{2,1,0:T(8,128)S(1)}, f32[2,512,128]{2,1,0:T(8,128)}, u32[]{:S(2)}) copy-start(f32[2,512,128]{2,1,0:T(8,128)} %constant.12.clone.turn_ref) | copy-start | bytes 1572868
  5.1 63.2 %copy-start.1 = (bf16[2,256,512]{2,1,0:T(8,128)(2,1)S(1)}, bf16[2,256,512]{2,1,0:T(8,128)(2,1)}, u32[]{:S(2)}) copy-start(bf16[2,256,512]{2,1,0:T(8,128)(2,1)} %constant.11.clone.t1i_ref) | copy-start | bytes 1572868
  5.1 63.2 %copy-start.2 = (bf16[2,512,256]{2,1,0:T(8,128)(2,1)S(1)}, bf16[2,512,256]{2,1,0:T(8,128)(2,1)}, u32[]{:S(2)}) copy-start(bf16[2,512,256]{2,1,0:T(8,128)(2,1)} %constant.10.clone.t1_ref) | copy-start | bytes 1572868
  5.1 63.2 %copy-start.3 = (bf16[256,256]{1,0:T(8,128)(2,1)S(1)}, bf16[256,256]{1,0:T(8,128)(2,1)}, u32[]{:S(2)}) copy-start(bf16[256,256]{1,0:T(8,128)(2,1)} %constant.14.clone.t2i_ref) | copy-start | bytes 393220
  5.1 63.2 %copy-start.4 = (bf16[256,256]{1,0:T(8,128)(2,1)S(1)}, bf16[256,256]{1,0:T(8,128)(2,1)}, u32[]{:S(2)}) copy-start(bf16[256,256]{1,0:T(8,128)(2,1)} %constant.13.clone.t2_ref) | copy-start | bytes 393220
  104.4 2.7 %collective-permute-start = (bf16[1024,128]{1,0:T(8,128)(2,1)S(1)}, bf16[1024,128]{1,0:T(8,128)(2,1)S(1)}, u32[]{:S(2)}, u32[]{:S(2)}) collective-permute-start(bf16[1024,128]{1,0:T(8,128)(2,1)S(1)} %shard_map.134.mine_ref), channel_id=1, source_target_pairs={{0,1},{1,0},{2,3},{3,2},{4,5},{5,4},{6,7},{7,6},{8,9},{9,8},{10,11... | collective-permute-start | bytes 786440 | tf_op jit(solution)/shard_map/ppermute | solution.py:397

commit v6 on v5

--- a/solution.py
+++ b/solution.py
@@ -206,17 +206,14 @@
         taps = half_turn(data[:, HALF - 1]) if d % 2 else data[:, HALF - 1]
         x_ref[rows, lanes(seqs + d // 2)] = taps.reshape(half, toks).astype(bf)
 
-    def forward(ref, count):
-        outs = [dot(t1_ref[n], ref[pl.ds(n * half, half), :]) for n in range(2)]
-        parts = []
-        for n in range(count):
-            re = jnp.concatenate([columns(out[:half], n) for out in outs], axis=0)
-            im = jnp.concatenate([columns(out[half:], n) for out in outs], axis=0)
-            parts.append(
-                jnp.concatenate([re * cosines + im * sines, im * cosines - re * sines], axis=1)
-                .astype(bf)
-            )
-        return dot(jnp.concatenate(parts, axis=0), t2_ref[...])
+    def first(ref):
+        return [dot(t1_ref[n], ref[pl.ds(n * half, half), :]) for n in range(2)]
+
+    def second(outs, n):
+        re = jnp.concatenate([columns(out[:half], n) for out in outs], axis=0)
+        im = jnp.concatenate([columns(out[half:], n) for out in outs], axis=0)
+        part = jnp.concatenate([re * cosines + im * sines, im * cosines - re * sines], axis=1)
+        return dot(part.astype(bf), t2_ref[...])
 
     def back(prod):
         re, im = columns(prod, 0), columns(prod, 1)
@@ -231,37 +228,42 @@
     def last(ref):
         return [dot(t1i_ref[n], ref[pl.ds(n * full, full), :]) for n in range(2)]
 
-    spec = forward(x_ref, seqs + 2)
-    spec_ref[...] = spec[:seqs * full]
-    for f in range(2):
-        taps = spec[(seqs + f) * full:(seqs + f + 1) * full]
-        tr, ti = columns(taps, 0), columns(taps, 1)
-        prods = []
-        for d in range(seqs):
-            ur = columns(spec[d * full:(d + 1) * full], 0)
-            ui = columns(spec[d * full:(d + 1) * full], 1)
-            prods.append(
-                jnp.concatenate([ur * tr - ui * ti, ur * ti + ui * tr], axis=1).astype(bf)
-            )
-        waves = dot(jnp.concatenate(prods, axis=0), t2i_ref[...])
-        for d in range(seqs):
-            keep(wave_ref, f * seqs + d, *back(waves[d * full:(d + 1) * full]))
-
-    conv = jnp.concatenate(last(wave_ref), axis=0).astype(bf).astype(f32)
+    outs = first(x_ref)
+    taps = [second(outs, seqs + f) for f in range(2)]
+    specs, waves = {}, {}
+    for d in range(seqs + 2):
+        if d < seqs:
+            specs[d] = second(outs, d)
+        if 0 <= d - 1 < seqs:
+            spec = specs[d - 1]
+            spec_ref[pl.ds((d - 1) * full, full), :] = spec
+            ur, ui = columns(spec, 0), columns(spec, 1)
+            for f in range(2):
+                tr, ti = columns(taps[f], 0), columns(taps[f], 1)
+                prod = jnp.concatenate([ur * tr - ui * ti, ur * ti + ui * tr], axis=1)
+                waves[d - 1, f] = dot(prod.astype(bf), t2i_ref[...])
+        if d >= 2:
+            for f in range(2):
+                keep(wave_ref, 2 * (d - 2) + f, *back(waves[d - 2, f]))
+
     for d in range(seqs):
         data = received(d)
-        gate_s = sets(data, 1)
-        stud = gate_s * columns(conv, seqs + d)
+        gate_s, gate_t = sets(data, 1), sets(data, 2)
+        conv = jnp.concatenate(
+            [dot(t1i_ref[n], wave_ref[pl.ds(n * full, full), pl.ds(2 * d * toks, 2 * toks)])
+             for n in range(2)], axis=0,
+        ).astype(bf).astype(f32)
+        conv_t, conv_s = columns(conv, 0), columns(conv, 1)
+        stud = gate_s * conv_s
         stud_ref[:, lanes(d)] = stud
-        grad = gate_s * (stud - sets(data, 2) * columns(conv, d))
-        grad_ref[:, lanes(d)] = grad.astype(bf)
-
-    spec = forward(grad_ref, seqs)
+        grad_ref[:, lanes(d)] = (gate_s * (stud - gate_t * conv_t)).astype(bf)
+
+    outs = first(grad_ref)
+    specs = [second(outs, d) for d in range(seqs)]
     sum_re = jnp.zeros((full, toks), f32)
     sum_im = jnp.zeros((full, toks), f32)
     for d in range(seqs):
-        gr = columns(spec[d * full:(d + 1) * full], 0)
-        gi = columns(spec[d * full:(d + 1) * full], 1)
+        gr, gi = columns(specs[d], 0), columns(specs[d], 1)
         ur = spec_ref[pl.ds(d * full, full), lanes(0)]
         ui = spec_ref[pl.ds(d * full, full), lanes(1)]
         sum_re += gr * ur + gi * ui

time: 108 us -> 108 us (level)
  no operation moved by 1% of the time
where the time goes in v6:
time: 108 us
  blocking collectives  94.3 us (87%)
  Pallas kernels  11.1 us (10%)
  starting transfers between devices  1.54 us (1%)
    all_to_all x2, blocking collectives, exchange(): lax.all_to_all(cut, ('dp', 'ctx'), split_axis=0, concat_axis=0, tiled=True)  94.3 us
    pallas_call x1, Pallas kernels, pack(): pl.pallas_call(functools.partial(pack_kernel, widths), in_specs=[pl.Block...  4.45 us
    pallas_call x1, Pallas kernels, filters(): pl.pallas_call(functools.partial(filter_kernel, seqs, blocks, scale), out...  4.4 us
  transfers between devices with their start and end apart: 1, of which 1 were waited for; matrix products, arithmetic and copies ran while one was open for 0% of the time, Pallas kernels for 1%

profile of v6, /device:TPU:1, one launch (start us, length us, event | category | flops | bytes accessed | tf_op | source)
XLA Modules:
  0.0 107.8 jit_solution(1049402957604552155)
XLA Ops:
  0.6 4.4 %shard_map.131 = bf16[7168,128]{1,0:T(8,128)(2,1)} custom-call(s32[1,128]{1,0:T(1,128)} %tok_ref.1, bf16[512,2048]{1,0:T(8,128)(2,1)} %emb_ref.1, bf16[1,128,2048]{2,1,0:T(8,128)(2,1)} %in_ref.1, bf16[1,128,2048]{2,1,0:T(8,128)(2,1)} %stud_ref.1, bf16[1,128,2048]{2,1,0:T(8,128)(2,1)} %teach_ref.1, bf16[128,2048]{1,0:T(8,128)(2,1)} %ft_ref.1, ...), custom_call_target="tpu_custom_call" | custom-call | tf_op jit(solution)/shard_map/pallas_call | solution.py:158
  5.1 0.0 copy-start
  5.1 0.0 copy-start.1
  5.1 0.0 copy-start.2
  5.1 0.0 copy-start.3
  5.1 0.0 copy-start.4
  5.2 63.1 %all_to_all.10 = bf16[256,7,4,128]{3,2,1,0:T(4,128)(2,1)S(1)} all-to-all(bf16[256,7,4,128]{3,2,1,0:T(4,128)(2,1)} %bitcast.8), channel_id=1, replica_groups=mesh['ctx'=64,'dp'=4] {'dp','ctx'}, dimensions={0} | all-to-all | bytes 3670016 | tf_op jit(solution)/shard_map/all_to_all | solution.py:394
  68.3 0.0 copy-done
  68.3 0.0 copy-done.1
  68.3 0.0 copy-done.2
  68.3 0.0 copy-done.3
  68.3 0.0 copy-done.4
  68.3 4.4 %shard_map.132 = bf16[3072,128]{1,0:T(8,128)(2,1)S(1)} custom-call(bf16[7168,128]{1,0:T(8,128)(2,1)S(1)} %bitcast.4, bf16[2,512,256]{2,1,0:T(8,128)(2,1)S(1)} %copy-done.2, bf16[2,256,512]{2,1,0:T(8,128)(2,1)S(1)} %copy-done.1, f32[2,512,128]{2,1,0:T(8,128)S(1)} %copy-done, bf16[256,256]{1,0:T(8,128)(2,1)S(1)} %copy-done.4, bf16[256,256]{1,0:T(8,128)(2,1)S(1)} %copy-done.3), custom_call_target="tpu_custom_call" | custom-call | tf_op jit(solution)/shard_map/pallas_call | solution.py:296
  72.7 31.2 %all_to_all.11 = bf16[256,3,4,128]{3,2,1,0:T(4,128)(2,1)S(1)} all-to-all(bf16[256,3,4,128]{3,2,1,0:T(4,128)(2,1)S(1)} %bitcast.7), channel_id=1, replica_groups=mesh['ctx'=64,'dp'=4] {'dp','ctx'}, dimensions={0} | all-to-all | bytes 1572864 | tf_op jit(solution)/shard_map/all_to_all | solution.py:394
  103.9 0.1 shard_map.134.mine_ref
  104.0 1.5 %collective-permute-start = (bf16[1024,128]{1,0:T(8,128)(2,1)S(1)}, bf16[1024,128]{1,0:T(8,128)(2,1)S(1)}, u32[]{:S(2)}, u32[]{:S(2)}) collective-permute-start(bf16[1024,128]{1,0:T(8,128)(2,1)S(1)} %shard_map.134.mine_ref), channel_id=1, source_target_pairs={{0,1},{1,0},{2,3},{3,2},{4,5},{5,4},{6,7},{7,6},{8,9},{9,8},{10,11... | collective-permute-start | bytes 786440 | tf_op jit(solution)/shard_map/ppermute | solution.py:399
  105.6 1.0 shard_map.133
  106.6 0.2 collective-permute-done.other_ref
  106.7 1.1 %shard_map.135 = f32[128,2048]{1,0:T(8,128)} custom-call(bf16[1024,128]{1,0:T(8,128)(2,1)S(1)} %shard_map.134.mine_ref, bf16[1024,128]{1,0:T(8,128)(2,1)S(1)} %collective-permute-done.other_ref), custom_call_target="tpu_custom_call" | custom-call | flops 1048576 | bytes 2097152 | tf_op jit(solution)/shard_map/pallas_call | solution.py:377
Async XLA Ops:
  5.1 63.2 %copy-start = (f32[2,512,128]{2,1,0:T(8,128)S(1)}, f32[2,512,128]{2,1,0:T(8,128)}, u32[]{:S(2)}) copy-start(f32[2,512,128]{2,1,0:T(8,128)} %constant.12.clone.turn_ref) | copy-start | bytes 1572868
  5.1 63.2 %copy-start.1 = (bf16[2,256,512]{2,1,0:T(8,128)(2,1)S(1)}, bf16[2,256,512]{2,1,0:T(8,128)(2,1)}, u32[]{:S(2)}) copy-start(bf16[2,256,512]{2,1,0:T(8,128)(2,1)} %constant.11.clone.t1i_ref) | copy-start | bytes 1572868
  5.1 63.2 %copy-start.2 = (bf16[2,512,256]{2,1,0:T(8,128)(2,1)S(1)}, bf16[2,512,256]{2,1,0:T(8,128)(2,1)}, u32[]{:S(2)}) copy-start(bf16[2,512,256]{2,1,0:T(8,128)(2,1)} %constant.10.clone.t1_ref) | copy-start | bytes 1572868
  5.1 63.2 %copy-start.3 = (bf16[256,256]{1,0:T(8,128)(2,1)S(1)}, bf16[256,256]{1,0:T(8,128)(2,1)}, u32[]{:S(2)}) copy-start(bf16[256,256]{1,0:T(8,128)(2,1)} %constant.14.clone.t2i_ref) | copy-start | bytes 393220
  5.1 63.2 %copy-start.4 = (bf16[256,256]{1,0:T(8,128)(2,1)S(1)}, bf16[256,256]{1,0:T(8,128)(2,1)}, u32[]{:S(2)}) copy-start(bf16[256,256]{1,0:T(8,128)(2,1)} %constant.13.clone.t2_ref) | copy-start | bytes 393220
  104.0 2.7 %collective-permute-start = (bf16[1024,128]{1,0:T(8,128)(2,1)S(1)}, bf16[1024,128]{1,0:T(8,128)(2,1)S(1)}, u32[]{:S(2)}, u32[]{:S(2)}) collective-permute-start(bf16[1024,128]{1,0:T(8,128)(2,1)S(1)} %shard_map.134.mine_ref), channel_id=1, source_target_pairs={{0,1},{1,0},{2,3},{3,2},{4,5},{5,4},{6,7},{7,6},{8,9},{9,8},{10,11... | collective-permute-start | bytes 786440 | tf_op jit(solution)/shard_map/ppermute | solution.py:399

commit v7 on v6

--- a/solution.py
+++ b/solution.py
@@ -61,7 +61,7 @@
 
 def pack_kernel(
     widths, tok_ref, emb_ref, in_ref, stud_ref, teach_ref, ft_ref, fs_ref, out_ref,
-    emb_buf, data_buf, out_buf, sems, out_sems,
+    emb_buf, data_buf, sems,
 ):
     vocab, channels = emb_ref.shape
     toks = tok_ref.shape[1]
@@ -116,7 +116,7 @@
         place = span(chunk)
 
         def store(tiles):
-            out_buf[place, :] = (
+            out_ref[place, :] = (
                 jnp.stack(tiles, axis=1).reshape(pairs * 2 * MESSAGE, toks).astype(jnp.bfloat16)
             )
 
@@ -138,16 +138,6 @@
                 halves(tap_upper, mix), halves(mix, stud), halves(stud, teach),
                 halves(teach, tap_lower),
             ] + [half_turn(x[:, 1]) for x in parts[:3]])
-
-        pltpu.make_async_copy(
-            out_buf.at[place, :], out_ref.at[place, :], out_sems.at[chunk]
-        ).start()
-
-    for chunk in range(chunks):
-        place = span(chunk)
-        pltpu.make_async_copy(
-            out_buf.at[place, :], out_ref.at[place, :], out_sems.at[chunk]
-        ).wait()
 
 
 def pack(token_ids, embedding, in_gate, teacher_gate, student_gate, teacher_filter, student_filter):
@@ -158,14 +148,12 @@
     return pl.pallas_call(
         functools.partial(pack_kernel, widths),
         in_specs=[pl.BlockSpec(memory_space=pltpu.VMEM)] + [here] * 6,
-        out_specs=here,
-        out_shape=jax.ShapeDtypeStruct((channels // SUB * MESSAGE, toks), jnp.bfloat16),
+        out_specs=pl.BlockSpec(memory_space=pltpu.VMEM),
+        out_shape=pltpu.VMEM((channels // SUB * MESSAGE, toks), jnp.bfloat16),
         scratch_shapes=[
             pltpu.VMEM((vocab, channels), jnp.bfloat16),
             pltpu.VMEM((4, toks, channels), jnp.bfloat16),
-            pltpu.VMEM((channels // SUB * MESSAGE, toks), jnp.bfloat16),
             pltpu.SemaphoreType.DMA((len(widths), 5)),
-            pltpu.SemaphoreType.DMA((len(widths),)),
         ],
         compiler_params=pltpu.CompilerParams(vmem_limit_bytes=60 * MIB),
     )(token_ids, embedding, in_gate, student_gate, teacher_gate, teacher_filter, student_filter)

time: 108 us -> 107 us (level)
  no operation moved by 1% of the time
where the time goes in v7:
time: 107 us
  blocking collectives  94.1 us (88%)
  Pallas kernels  10.3 us (10%)
  starting transfers between devices  1.54 us (1%)
    all_to_all x2, blocking collectives, exchange(): lax.all_to_all(cut, ('dp', 'ctx'), split_axis=0, concat_axis=0, tiled=True)  94.1 us
    pallas_call x1, Pallas kernels, filters(): pl.pallas_call(functools.partial(filter_kernel, seqs, blocks, scale), out...  4.4 us
    pallas_call x1, Pallas kernels, pack(): pl.pallas_call(functools.partial(pack_kernel, widths), in_specs=[pl.Block...  3.65 us
  transfers between devices with their start and end apart: 1, of which 1 were waited for; matrix products, arithmetic and copies ran while one was open for 0% of the time, Pallas kernels for 1%

profile of v7, /device:TPU:1, one launch (start us, length us, event | category | flops | bytes accessed | tf_op | source)
XLA Modules:
  0.0 106.8 jit_solution(2942561029638378318)
XLA Ops:
  0.6 3.6 %shard_map.131 = bf16[7168,128]{1,0:T(8,128)(2,1)S(1)} custom-call(s32[1,128]{1,0:T(1,128)} %tok_ref.1, bf16[512,2048]{1,0:T(8,128)(2,1)} %emb_ref.1, bf16[1,128,2048]{2,1,0:T(8,128)(2,1)} %in_ref.1, bf16[1,128,2048]{2,1,0:T(8,128)(2,1)} %stud_ref.1, bf16[1,128,2048]{2,1,0:T(8,128)(2,1)} %teach_ref.1, bf16[128,2048]{1,0:T(8,128)(2,1)} %ft_ref.1, ...), custom_call_target="tpu_custom_call" | custom-call | tf_op jit(solution)/shard_map/pallas_call | solution.py:148
  4.3 0.0 copy-start
  4.3 0.0 copy-start.1
  4.3 0.0 copy-start.2
  4.3 0.0 copy-start.3
  4.3 0.0 copy-start.4
  4.4 62.9 %all_to_all.10 = bf16[256,7,4,128]{3,2,1,0:T(4,128)(2,1)S(1)} all-to-all(bf16[256,7,4,128]{3,2,1,0:T(4,128)(2,1)S(1)} %bitcast.5), channel_id=1, replica_groups=mesh['ctx'=64,'dp'=4] {'dp','ctx'}, dimensions={0} | all-to-all | bytes 3670016 | tf_op jit(solution)/shard_map/all_to_all | solution.py:382
  67.3 0.0 copy-done
  67.3 0.0 copy-done.1
  67.3 0.0 copy-done.2
  67.3 0.0 copy-done.3
  67.3 0.0 copy-done.4
  67.3 4.4 %shard_map.132 = bf16[3072,128]{1,0:T(8,128)(2,1)S(1)} custom-call(bf16[7168,128]{1,0:T(8,128)(2,1)S(1)} %bitcast.4, bf16[2,512,256]{2,1,0:T(8,128)(2,1)S(1)} %copy-done.2, bf16[2,256,512]{2,1,0:T(8,128)(2,1)S(1)} %copy-done.1, f32[2,512,128]{2,1,0:T(8,128)S(1)} %copy-done, bf16[256,256]{1,0:T(8,128)(2,1)S(1)} %copy-done.4, bf16[256,256]{1,0:T(8,128)(2,1)S(1)} %copy-done.3), custom_call_target="tpu_custom_call" | custom-call | tf_op jit(solution)/shard_map/pallas_call | solution.py:284
  71.7 31.2 %all_to_all.11 = bf16[256,3,4,128]{3,2,1,0:T(4,128)(2,1)S(1)} all-to-all(bf16[256,3,4,128]{3,2,1,0:T(4,128)(2,1)S(1)} %bitcast.8), channel_id=1, replica_groups=mesh['ctx'=64,'dp'=4] {'dp','ctx'}, dimensions={0} | all-to-all | bytes 1572864 | tf_op jit(solution)/shard_map/all_to_all | solution.py:382
  102.9 0.1 shard_map.134.mine_ref
  103.0 1.5 %collective-permute-start = (bf16[1024,128]{1,0:T(8,128)(2,1)S(1)}, bf16[1024,128]{1,0:T(8,128)(2,1)S(1)}, u32[]{:S(2)}, u32[]{:S(2)}) collective-permute-start(bf16[1024,128]{1,0:T(8,128)(2,1)S(1)} %shard_map.134.mine_ref), channel_id=1, source_target_pairs={{0,1},{1,0},{2,3},{3,2},{4,5},{5,4},{6,7},{7,6},{8,9},{9,8},{10,11... | collective-permute-start | bytes 786440 | tf_op jit(solution)/shard_map/ppermute | solution.py:387
  104.6 1.0 shard_map.133
  105.6 0.2 collective-permute-done.other_ref
  105.7 1.1 %shard_map.135 = f32[128,2048]{1,0:T(8,128)} custom-call(bf16[1024,128]{1,0:T(8,128)(2,1)S(1)} %shard_map.134.mine_ref, bf16[1024,128]{1,0:T(8,128)(2,1)S(1)} %collective-permute-done.other_ref), custom_call_target="tpu_custom_call" | custom-call | flops 1048576 | bytes 2097152 | tf_op jit(solution)/shard_map/pallas_call | solution.py:365
Async XLA Ops:
  4.3 63.0 %copy-start = (f32[2,512,128]{2,1,0:T(8,128)S(1)}, f32[2,512,128]{2,1,0:T(8,128)}, u32[]{:S(2)}) copy-start(f32[2,512,128]{2,1,0:T(8,128)} %constant.12.clone.turn_ref) | copy-start | bytes 1572868
  4.3 63.0 %copy-start.1 = (bf16[2,256,512]{2,1,0:T(8,128)(2,1)S(1)}, bf16[2,256,512]{2,1,0:T(8,128)(2,1)}, u32[]{:S(2)}) copy-start(bf16[2,256,512]{2,1,0:T(8,128)(2,1)} %constant.11.clone.t1i_ref) | copy-start | bytes 1572868
  4.3 63.0 %copy-start.2 = (bf16[2,512,256]{2,1,0:T(8,128)(2,1)S(1)}, bf16[2,512,256]{2,1,0:T(8,128)(2,1)}, u32[]{:S(2)}) copy-start(bf16[2,512,256]{2,1,0:T(8,128)(2,1)} %constant.10.clone.t1_ref) | copy-start | bytes 1572868
  4.3 62.9 %copy-start.3 = (bf16[256,256]{1,0:T(8,128)(2,1)S(1)}, bf16[256,256]{1,0:T(8,128)(2,1)}, u32[]{:S(2)}) copy-start(bf16[256,256]{1,0:T(8,128)(2,1)} %constant.14.clone.t2i_ref) | copy-start | bytes 393220
  4.3 62.9 %copy-start.4 = (bf16[256,256]{1,0:T(8,128)(2,1)S(1)}, bf16[256,256]{1,0:T(8,128)(2,1)}, u32[]{:S(2)}) copy-start(bf16[256,256]{1,0:T(8,128)(2,1)} %constant.13.clone.t2_ref) | copy-start | bytes 393220
  103.0 2.7 %collective-permute-start = (bf16[1024,128]{1,0:T(8,128)(2,1)S(1)}, bf16[1024,128]{1,0:T(8,128)(2,1)S(1)}, u32[]{:S(2)}, u32[]{:S(2)}) collective-permute-start(bf16[1024,128]{1,0:T(8,128)(2,1)S(1)} %shard_map.134.mine_ref), channel_id=1, source_target_pairs={{0,1},{1,0},{2,3},{3,2},{4,5},{5,4},{6,7},{7,6},{8,9},{9,8},{10,11... | collective-permute-start | bytes 786440 | tf_op jit(solution)/shard_map/ppermute | solution.py:387

commit v8 on v7

--- a/solution.py
+++ b/solution.py
@@ -308,13 +308,35 @@
     return both.astype(jnp.bfloat16).T
 
 
-def student_kernel(in_ref, out_ref):
+def leave(out_ref, buf, sems, parts, count):
+    width = buf.shape[1] // parts
+    copies = []
+    for n in range(parts):
+        cols = pl.ds(n * width, width)
+        buf[:, cols] = count(n)
+        copies.append(pltpu.make_async_copy(buf.at[:, cols], out_ref.at[:, cols], sems.at[n]))
+        copies[-1].start()
+    for copy in copies:
+        copy.wait()
+
+
+def cut(x, n, parts):
+    size = x.shape[0] // parts
+    return x[n * size:(n + 1) * size]
+
+
+def student_kernel(parts, in_ref, out_ref, buf, sems):
     even = lax.rem(lax.axis_index("ctx"), 2) == 0
-    first, middle, last = tiles(in_ref)
-    turned_last = half_turn(last)
-    upper = jnp.where(even, first, halves(middle, first))
-    lower = jnp.where(even, halves(half_turn(middle), turned_last), turned_last)
-    out_ref[0] = channels(upper, lower)
+    rows = in_ref.shape[0] // parts
+
+    def count(n):
+        first, middle, last = tiles(in_ref.at[pl.ds(n * rows, rows), :])
+        turned_last = half_turn(last)
+        upper = jnp.where(even, first, halves(middle, first))
+        lower = jnp.where(even, halves(half_turn(middle), turned_last), turned_last)
+        return channels(upper, lower)
+
+    leave(out_ref.at[0], buf, sems, parts, count)
 
 
 def pick_kernel(in_ref, out_ref):
@@ -324,26 +346,29 @@
     out_ref[...] = taps.reshape(out_ref.shape).astype(jnp.bfloat16)
 
 
-def lags_kernel(mine_ref, other_ref, out_ref):
+def lags_kernel(parts, mine_ref, other_ref, out_ref, buf, sems):
     lead = lax.rem(lax.axis_index("dp"), 2) == 0
     rows, toks = mine_ref.shape
-    mine, other = [
-        ref[...].astype(jnp.float32).reshape(rows // SUB, SUB, toks)
-        for ref in (mine_ref, other_ref)
-    ]
-    upper = jnp.where(lead, mine, other)
-    lower = jnp.where(lead, other, mine)
-    out_ref[...] = channels(
-        halves(upper, half_turn(lower)), halves(half_turn(upper), lower)
-    ).astype(jnp.float32)
+    rows //= parts
+
+    def count(n):
+        mine, other = [
+            ref[pl.ds(n * rows, rows), :].astype(jnp.float32).reshape(rows // SUB, SUB, toks)
+            for ref in (mine_ref, other_ref)
+        ]
+        upper = jnp.where(lead, mine, other)
+        lower = jnp.where(lead, other, mine)
+        return channels(
+            halves(upper, half_turn(lower)), halves(half_turn(upper), lower)
+        ).astype(jnp.float32)
+
+    leave(out_ref, buf, sems, parts, count)
 
 
 def unpack(got, swap):
     rows, toks = got.shape
     count = rows // REPLY * SUB
-    width = 1024
-    message = pl.BlockSpec((width // SUB * REPLY, toks), lambda g: (g, 0))
-    picked = pl.BlockSpec((width // 2, toks), lambda g: (g, 0))
+    parts = 4
     params = pltpu.CompilerParams(vmem_limit_bytes=32 * MIB)
     size = pl.CostEstimate(flops=MIB, bytes_accessed=2 * MIB, transcendentals=0)
     mine = pl.pallas_call(
@@ -354,19 +379,23 @@
     )(got)
     other = swap(mine)
     student = pl.pallas_call(
-        student_kernel,
-        grid=(count // width,),
-        in_specs=[message],
-        out_specs=pl.BlockSpec((1, toks, width), lambda g: (0, 0, g)),
+        functools.partial(student_kernel, parts),
+        in_specs=[pl.BlockSpec(memory_space=pltpu.VMEM)],
+        out_specs=pl.BlockSpec(memory_space=pl.ANY),
+        scratch_shapes=[
+            pltpu.VMEM((toks, count), jnp.bfloat16), pltpu.SemaphoreType.DMA((parts,)),
+        ],
         out_shape=jax.ShapeDtypeStruct((1, toks, count), jnp.bfloat16),
         compiler_params=params,
         cost_estimate=size,
     )(got)
     lags = pl.pallas_call(
-        lags_kernel,
-        grid=(count // width,),
-        in_specs=[picked, picked],
-        out_specs=pl.BlockSpec((toks, width), lambda g: (0, g)),
+        functools.partial(lags_kernel, parts),
+        in_specs=[pl.BlockSpec(memory_space=pltpu.VMEM)] * 2,
+        out_specs=pl.BlockSpec(memory_space=pl.ANY),
+        scratch_shapes=[
+            pltpu.VMEM((toks, count), jnp.float32), pltpu.SemaphoreType.DMA((parts,)),
+        ],
         out_shape=jax.ShapeDtypeStruct((toks, count), jnp.float32),
         compiler_params=params,
         cost_estimate=size,

time: 107 us -> 107 us (level)
  no operation moved by 1% of the time
where the time goes in v8:
time: 107 us
  blocking collectives  94.1 us (88%)
  Pallas kernels  10.2 us (10%)
  starting transfers between devices  1.54 us (1%)
    all_to_all x2, blocking collectives, exchange(): lax.all_to_all(cut, ('dp', 'ctx'), split_axis=0, concat_axis=0, tiled=True)  94.1 us
    pallas_call x1, Pallas kernels, filters(): pl.pallas_call(functools.partial(filter_kernel, seqs, blocks, scale), out...  4.4 us
    pallas_call x1, Pallas kernels, pack(): pl.pallas_call(functools.partial(pack_kernel, widths), in_specs=[pl.Block...  3.65 us
  transfers between devices with their start and end apart: 1, of which 1 were waited for; matrix products, arithmetic and copies ran while one was open for 0% of the time, Pallas kernels for 1%

profile of v8, /device:TPU:1, one launch (start us, length us, event | category | flops | bytes accessed | tf_op | source)
XLA Modules:
  0.0 106.8 jit_solution(14004258439470135545)
XLA Ops:
  0.6 3.6 %shard_map.131 = bf16[7168,128]{1,0:T(8,128)(2,1)S(1)} custom-call(s32[1,128]{1,0:T(1,128)} %tok_ref.1, bf16[512,2048]{1,0:T(8,128)(2,1)} %emb_ref.1, bf16[1,128,2048]{2,1,0:T(8,128)(2,1)} %in_ref.1, bf16[1,128,2048]{2,1,0:T(8,128)(2,1)} %stud_ref.1, bf16[1,128,2048]{2,1,0:T(8,128)(2,1)} %teach_ref.1, bf16[128,2048]{1,0:T(8,128)(2,1)} %ft_ref.1, ...), custom_call_target="tpu_custom_call" | custom-call | tf_op jit(solution)/shard_map/pallas_call | solution.py:148
  4.3 0.0 copy-start
  4.3 0.0 copy-start.1
  4.3 0.0 copy-start.2
  4.3 0.0 copy-start.3
  4.3 0.0 copy-start.4
  4.4 62.9 %all_to_all.10 = bf16[256,7,4,128]{3,2,1,0:T(4,128)(2,1)S(1)} all-to-all(bf16[256,7,4,128]{3,2,1,0:T(4,128)(2,1)S(1)} %bitcast.5), channel_id=1, replica_groups=mesh['ctx'=64,'dp'=4] {'dp','ctx'}, dimensions={0} | all-to-all | bytes 3670016 | tf_op jit(solution)/shard_map/all_to_all | solution.py:411
  67.3 0.0 copy-done
  67.3 0.0 copy-done.1
  67.3 0.0 copy-done.2
  67.3 0.0 copy-done.3
  67.3 0.0 copy-done.4
  67.3 4.4 %shard_map.132 = bf16[3072,128]{1,0:T(8,128)(2,1)S(1)} custom-call(bf16[7168,128]{1,0:T(8,128)(2,1)S(1)} %bitcast.4, bf16[2,512,256]{2,1,0:T(8,128)(2,1)S(1)} %copy-done.2, bf16[2,256,512]{2,1,0:T(8,128)(2,1)S(1)} %copy-done.1, f32[2,512,128]{2,1,0:T(8,128)S(1)} %copy-done, bf16[256,256]{1,0:T(8,128)(2,1)S(1)} %copy-done.4, bf16[256,256]{1,0:T(8,128)(2,1)S(1)} %copy-done.3), custom_call_target="tpu_custom_call" | custom-call | tf_op jit(solution)/shard_map/pallas_call | solution.py:284
  71.7 31.2 %all_to_all.11 = bf16[256,3,4,128]{3,2,1,0:T(4,128)(2,1)S(1)} all-to-all(bf16[256,3,4,128]{3,2,1,0:T(4,128)(2,1)S(1)} %bitcast.8), channel_id=1, replica_groups=mesh['ctx'=64,'dp'=4] {'dp','ctx'}, dimensions={0} | all-to-all | bytes 1572864 | tf_op jit(solution)/shard_map/all_to_all | solution.py:411
  102.9 0.1 shard_map.134.mine_ref
  103.0 1.5 %collective-permute-start = (bf16[1024,128]{1,0:T(8,128)(2,1)S(1)}, bf16[1024,128]{1,0:T(8,128)(2,1)S(1)}, u32[]{:S(2)}, u32[]{:S(2)}) collective-permute-start(bf16[1024,128]{1,0:T(8,128)(2,1)S(1)} %shard_map.134.mine_ref), channel_id=1, source_target_pairs={{0,1},{1,0},{2,3},{3,2},{4,5},{5,4},{6,7},{7,6},{8,9},{9,8},{10,11... | collective-permute-start | bytes 786440 | tf_op jit(solution)/shard_map/ppermute | solution.py:416
  104.6 0.9 shard_map.133
  105.5 0.2 collective-permute-done.other_ref
  105.7 1.1 %shard_map.135 = f32[128,2048]{1,0:T(8,128)} custom-call(bf16[1024,128]{1,0:T(8,128)(2,1)S(1)} %shard_map.134.mine_ref, bf16[1024,128]{1,0:T(8,128)(2,1)S(1)} %collective-permute-done.other_ref), custom_call_target="tpu_custom_call" | custom-call | flops 1048576 | bytes 2097152 | tf_op jit(solution)/shard_map/pallas_call | solution.py:392
Async XLA Ops:
  4.3 63.0 %copy-start = (f32[2,512,128]{2,1,0:T(8,128)S(1)}, f32[2,512,128]{2,1,0:T(8,128)}, u32[]{:S(2)}) copy-start(f32[2,512,128]{2,1,0:T(8,128)} %constant.12.clone.turn_ref) | copy-start | bytes 1572868
  4.3 63.0 %copy-start.1 = (bf16[2,256,512]{2,1,0:T(8,128)(2,1)S(1)}, bf16[2,256,512]{2,1,0:T(8,128)(2,1)}, u32[]{:S(2)}) copy-start(bf16[2,256,512]{2,1,0:T(8,128)(2,1)} %constant.11.clone.t1i_ref) | copy-start | bytes 1572868
  4.3 63.0 %copy-start.2 = (bf16[2,512,256]{2,1,0:T(8,128)(2,1)S(1)}, bf16[2,512,256]{2,1,0:T(8,128)(2,1)}, u32[]{:S(2)}) copy-start(bf16[2,512,256]{2,1,0:T(8,128)(2,1)} %constant.10.clone.t1_ref) | copy-start | bytes 1572868
  4.3 62.9 %copy-start.3 = (bf16[256,256]{1,0:T(8,128)(2,1)S(1)}, bf16[256,256]{1,0:T(8,128)(2,1)}, u32[]{:S(2)}) copy-start(bf16[256,256]{1,0:T(8,128)(2,1)} %constant.14.clone.t2i_ref) | copy-start | bytes 393220
  4.3 62.9 %copy-start.4 = (bf16[256,256]{1,0:T(8,128)(2,1)S(1)}, bf16[256,256]{1,0:T(8,128)(2,1)}, u32[]{:S(2)}) copy-start(bf16[256,256]{1,0:T(8,128)(2,1)} %constant.13.clone.t2_ref) | copy-start | bytes 393220
  103.0 2.7 %collective-permute-start = (bf16[1024,128]{1,0:T(8,128)(2,1)S(1)}, bf16[1024,128]{1,0:T(8,128)(2,1)S(1)}, u32[]{:S(2)}, u32[]{:S(2)}) collective-permute-start(bf16[1024,128]{1,0:T(8,128)(2,1)S(1)} %shard_map.134.mine_ref), channel_id=1, source_target_pairs={{0,1},{1,0},{2,3},{3,2},{4,5},{5,4},{6,7},{7,6},{8,9},{9,8},{10,11... | collective-permute-start | bytes 786440 | tf_op jit(solution)/shard_map/ppermute | solution.py:416

commit v9 on v8

--- a/solution.py
+++ b/solution.py
@@ -143,7 +143,7 @@
 def pack(token_ids, embedding, in_gate, teacher_gate, student_gate, teacher_filter, student_filter):
     vocab, channels = embedding.shape
     toks = token_ids.shape[1]
-    widths = (512,) * (channels // 512)
+    widths = (channels * 5 // 8, channels * 3 // 8)
     here = pl.BlockSpec(memory_space=pl.ANY)
     return pl.pallas_call(
         functools.partial(pack_kernel, widths),

time: 107 us -> 107 us (level)
  no operation moved by 1% of the time
where the time goes in v9:
time: 107 us
  blocking collectives  94.1 us (88%)
  Pallas kernels  10.1 us (9%)
  starting transfers between devices  1.54 us (1%)
    all_to_all x2, blocking collectives, exchange(): lax.all_to_all(cut, ('dp', 'ctx'), split_axis=0, concat_axis=0, tiled=True)  94.1 us
    pallas_call x1, Pallas kernels, filters(): pl.pallas_call(functools.partial(filter_kernel, seqs, blocks, scale), out...  4.41 us
    pallas_call x1, Pallas kernels, pack(): pl.pallas_call(functools.partial(pack_kernel, widths), in_specs=[pl.Block...  3.55 us
  transfers between devices with their start and end apart: 1, of which 1 were waited for; matrix products, arithmetic and copies ran while one was open for 0% of the time, Pallas kernels for 1%

profile of v9, /device:TPU:1, one launch (start us, length us, event | category | flops | bytes accessed | tf_op | source)
XLA Modules:
  0.0 106.7 jit_solution(6562633966251903250)
XLA Ops:
  0.6 3.5 %shard_map.131 = bf16[7168,128]{1,0:T(8,128)(2,1)S(1)} custom-call(s32[1,128]{1,0:T(1,128)} %tok_ref.1, bf16[512,2048]{1,0:T(8,128)(2,1)} %emb_ref.1, bf16[1,128,2048]{2,1,0:T(8,128)(2,1)} %in_ref.1, bf16[1,128,2048]{2,1,0:T(8,128)(2,1)} %stud_ref.1, bf16[1,128,2048]{2,1,0:T(8,128)(2,1)} %teach_ref.1, bf16[128,2048]{1,0:T(8,128)(2,1)} %ft_ref.1, ...), custom_call_target="tpu_custom_call" | custom-call | tf_op jit(solution)/shard_map/pallas_call | solution.py:148
  4.2 0.0 copy-start
  4.2 0.0 copy-start.1
  4.2 0.0 copy-start.2
  4.2 0.0 copy-start.3
  4.2 0.0 copy-start.4
  4.3 62.9 %all_to_all.10 = bf16[256,7,4,128]{3,2,1,0:T(4,128)(2,1)S(1)} all-to-all(bf16[256,7,4,128]{3,2,1,0:T(4,128)(2,1)S(1)} %bitcast.5), channel_id=1, replica_groups=mesh['ctx'=64,'dp'=4] {'dp','ctx'}, dimensions={0} | all-to-all | bytes 3670016 | tf_op jit(solution)/shard_map/all_to_all | solution.py:411
  67.1 0.0 copy-done
  67.2 0.0 copy-done.1
  67.2 0.0 copy-done.2
  67.2 0.0 copy-done.3
  67.2 0.0 copy-done.4
  67.2 4.4 %shard_map.132 = bf16[3072,128]{1,0:T(8,128)(2,1)S(1)} custom-call(bf16[7168,128]{1,0:T(8,128)(2,1)S(1)} %bitcast.4, bf16[2,512,256]{2,1,0:T(8,128)(2,1)S(1)} %copy-done.2, bf16[2,256,512]{2,1,0:T(8,128)(2,1)S(1)} %copy-done.1, f32[2,512,128]{2,1,0:T(8,128)S(1)} %copy-done, bf16[256,256]{1,0:T(8,128)(2,1)S(1)} %copy-done.4, bf16[256,256]{1,0:T(8,128)(2,1)S(1)} %copy-done.3), custom_call_target="tpu_custom_call" | custom-call | tf_op jit(solution)/shard_map/pallas_call | solution.py:284
  71.6 31.2 %all_to_all.11 = bf16[256,3,4,128]{3,2,1,0:T(4,128)(2,1)S(1)} all-to-all(bf16[256,3,4,128]{3,2,1,0:T(4,128)(2,1)S(1)} %bitcast.8), channel_id=1, replica_groups=mesh['ctx'=64,'dp'=4] {'dp','ctx'}, dimensions={0} | all-to-all | bytes 1572864 | tf_op jit(solution)/shard_map/all_to_all | solution.py:411
  102.8 0.1 shard_map.134.mine_ref
  102.9 1.5 %collective-permute-start = (bf16[1024,128]{1,0:T(8,128)(2,1)S(1)}, bf16[1024,128]{1,0:T(8,128)(2,1)S(1)}, u32[]{:S(2)}, u32[]{:S(2)}) collective-permute-start(bf16[1024,128]{1,0:T(8,128)(2,1)S(1)} %shard_map.134.mine_ref), channel_id=1, source_target_pairs={{0,1},{1,0},{2,3},{3,2},{4,5},{5,4},{6,7},{7,6},{8,9},{9,8},{10,11... | collective-permute-start | bytes 786440 | tf_op jit(solution)/shard_map/ppermute | solution.py:416
  104.4 0.9 shard_map.133
  105.4 0.2 collective-permute-done.other_ref
  105.6 1.1 %shard_map.135 = f32[128,2048]{1,0:T(8,128)} custom-call(bf16[1024,128]{1,0:T(8,128)(2,1)S(1)} %shard_map.134.mine_ref, bf16[1024,128]{1,0:T(8,128)(2,1)S(1)} %collective-permute-done.other_ref), custom_call_target="tpu_custom_call" | custom-call | flops 1048576 | bytes 2097152 | tf_op jit(solution)/shard_map/pallas_call | solution.py:392
Async XLA Ops:
  4.2 63.0 %copy-start = (f32[2,512,128]{2,1,0:T(8,128)S(1)}, f32[2,512,128]{2,1,0:T(8,128)}, u32[]{:S(2)}) copy-start(f32[2,512,128]{2,1,0:T(8,128)} %constant.12.clone.turn_ref) | copy-start | bytes 1572868
  4.2 63.0 %copy-start.1 = (bf16[2,256,512]{2,1,0:T(8,128)(2,1)S(1)}, bf16[2,256,512]{2,1,0:T(8,128)(2,1)}, u32[]{:S(2)}) copy-start(bf16[2,256,512]{2,1,0:T(8,128)(2,1)} %constant.11.clone.t1i_ref) | copy-start | bytes 1572868
  4.2 62.9 %copy-start.2 = (bf16[2,512,256]{2,1,0:T(8,128)(2,1)S(1)}, bf16[2,512,256]{2,1,0:T(8,128)(2,1)}, u32[]{:S(2)}) copy-start(bf16[2,512,256]{2,1,0:T(8,128)(2,1)} %constant.10.clone.t1_ref) | copy-start | bytes 1572868
  4.2 62.9 %copy-start.3 = (bf16[256,256]{1,0:T(8,128)(2,1)S(1)}, bf16[256,256]{1,0:T(8,128)(2,1)}, u32[]{:S(2)}) copy-start(bf16[256,256]{1,0:T(8,128)(2,1)} %constant.14.clone.t2i_ref) | copy-start | bytes 393220
  4.2 62.9 %copy-start.4 = (bf16[256,256]{1,0:T(8,128)(2,1)S(1)}, bf16[256,256]{1,0:T(8,128)(2,1)}, u32[]{:S(2)}) copy-start(bf16[256,256]{1,0:T(8,128)(2,1)} %constant.13.clone.t2_ref) | copy-start | bytes 393220
  102.9 2.7 %collective-permute-start = (bf16[1024,128]{1,0:T(8,128)(2,1)S(1)}, bf16[1024,128]{1,0:T(8,128)(2,1)S(1)}, u32[]{:S(2)}, u32[]{:S(2)}) collective-permute-start(bf16[1024,128]{1,0:T(8,128)(2,1)S(1)} %shard_map.134.mine_ref), channel_id=1, source_target_pairs={{0,1},{1,0},{2,3},{3,2},{4,5},{5,4},{6,7},{7,6},{8,9},{9,8},{10,11... | collective-permute-start | bytes 786440 | tf_op jit(solution)/shard_map/ppermute | solution.py:416
